TPU v7x, 32 devices: a whole 2x2x4 slice. The times are simulated.
32 devices in a mesh: dom: 8 (over z, core), blk: 4 (over y, x).
Axes of the slice: x: 2, y: 2, z: 4, core: 2. Of those that a mesh axis runs over, the one named last changes fastest.
Arguments:
- images: bfloat16 [512, 128, 256], P('dom', 'blk'), may hold values from -4.5 to 6.5
- ref_store: bfloat16 [8, 16, 4, 128, 256], P('dom', None, None, 'blk'), may hold values from -0.03125 to 0.03125
- block_owner: int32 [16], replicated, may hold values from 0 to 7, as said below
- class_gain: float32 [64], replicated, may hold values from 0.5 to 2
- precision: float32 [512], P('dom'), may hold values from 0.5 to 80
Outputs:
- class_sums: float32 [8, 2, 4, 128, 256], P('dom', None, None, 'blk')
Inputs may be any that keep to these rules, and one draw needn't show every extreme that they name: `block_owner`: each index d of dom owns exactly 2 blocks.
All inputs are finite; a program needn't handle non-finite values.
Results may differ from a plain program's by a relative error of at most 0.0049.
Values may be sent and summed in bfloat16 or wider, within the bound.
A program may use at most 64 MiB of HBM per device.

v0:
```python
import jax
import jax.numpy as jnp
from jax import lax
from jax.sharding import PartitionSpec as P

S = 64
SG = 4


def shards(images, ref_store, block_owner, class_gain, precision):
    particles = images.shape[0]
    cycle_count = images.shape[1]
    angles = images.shape[2]
    block_count = block_owner.shape[0]
    per_block = ref_store.shape[2]
    classes = block_count * per_block
    rot_step = angles // S
    stored_here = ref_store[0]
    owned_count = block_count // lax.axis_size("dom")
    owner_order = jnp.argsort(block_owner, stable=True)
    start_pos = lax.axis_index("dom") * owned_count
    mine = lax.dynamic_slice_in_dim(owner_order, start_pos, owned_count, 0)
    owned_blocks = jnp.take(stored_here, mine, axis=0)
    gathered = lax.all_gather(owned_blocks, "dom", axis=0, tiled=True)
    position = jnp.argsort(owner_order, stable=True)
    stored = jnp.take(gathered, position, axis=0)
    references = (
        stored.astype(jnp.float32) * class_gain.reshape(block_count, per_block, 1, 1)
    ).astype(jnp.bfloat16)
    ref_cube = references.reshape(classes, cycle_count, angles)
    ref_float = ref_cube.astype(jnp.float32)
    norm_part = jnp.sum(ref_float * ref_float, axis=(1, 2))
    flat_images = images.reshape(particles, cycle_count * angles)
    image_float = flat_images.astype(jnp.float32)
    doubled = jnp.concatenate([ref_cube, ref_cube], axis=2)
    groups = S // SG
    group_span = rot_step * SG

    def correlate(group_index, buffer):
        window = lax.dynamic_slice_in_dim(doubled, group_index * group_span, angles + group_span, 2)
        rolled = jnp.stack(
            [
                window[:, :, shift_index * rot_step : shift_index * rot_step + angles]
                for shift_index in range(SG)
            ],
            0,
        )
        rolled = rolled.reshape(SG * classes, cycle_count * angles)
        products = lax.dot_general(
            flat_images, rolled, (((1,), (1,)), ((), ())), preferred_element_type=jnp.float32
        )
        return lax.dynamic_update_index_in_dim(buffer, products, group_index, 0)

    scores = lax.fori_loop(
        0, groups, correlate, jnp.zeros((groups, particles, SG * classes), jnp.float32)
    )
    row_scale = precision[None, :, None]
    total_scores, total_norms = lax.psum((scores, norm_part), "blk")
    logits = row_scale * (total_scores - 0.5 * jnp.tile(total_norms, SG)[None, None, :])
    row_max = jnp.max(logits, axis=(0, 2), keepdims=True)
    exponent = jnp.exp(logits - row_max)
    weights = exponent / jnp.sum(exponent, axis=(0, 2), keepdims=True)

    def accumulate(counter, running):
        group_index = groups - 1 - counter
        group_weights = lax.dynamic_index_in_dim(weights, group_index, 0, keepdims=False)
        spread = lax.dot_general(
            group_weights,
            image_float,
            (((0,), (0,)), ((), ())),
            precision=lax.Precision.HIGHEST,
            preferred_element_type=jnp.float32,
        )
        spread = spread.reshape(SG, classes, cycle_count, angles)
        for shift_index in reversed(range(SG)):
            running = jnp.roll(running, rot_step, axis=2) + spread[shift_index]
        return running

    totals = lax.fori_loop(
        0, groups, accumulate, jnp.zeros((classes, cycle_count, angles), jnp.float32)
    )
    final_order = jnp.argsort(block_owner, stable=True)
    blocked = jnp.take(
        totals.reshape(block_count, per_block, cycle_count, angles), final_order, axis=0
    )
    owned_totals = lax.psum_scatter(blocked, "dom", scatter_dimension=0, tiled=True)
    return owned_totals[None]


def solution(mesh):
    return jax.shard_map(
        shards,
        mesh=mesh,
        in_specs=(P("dom", "blk", None), P("dom", None, None, "blk", None), P(), P(), P("dom")),
        out_specs=P("dom", None, None, "blk", None),
        check_vma=False,
    )
```

profile of v0, /device:TPU:0, one launch (start us, length us, event | category | flops | bytes accessed | tf_op | source)
XLA Modules:
  0.0 666.5 jit_solution(922508498244291265)
XLA Ops:
  14.4 20.5 %all-gather.2.cloned.1.call-done = bf16[16,4,32,256]{3,2,1,0:T(8,128)(2,1)} async-done(((bf16[2,4,32,256]{3,2,1,0:T(8,128)(2,1)}), bf16[16,4,32,256]{3,2,1,0:T(8,128)(2,1)}) %all-gather.2.cloned.1.call-update) | async-done | bytes 1048592 | tf_op jit(solution)/shard_map/all_gather | solution.py:24
  37.8 144.8 %while.29 = (s32[]{:T(128)}, f32[16,64,256]{2,1,0:T(8,128)}, bf16[64,32,512]{2,1,0:T(8,128)(2,1)S(1)}, bf16[64,8192]{1,0:T(8,128)(2,1)}, s32[]{:T(128)}, /*index...) while((s32[]{:T(128)}, f32[16,64,256]{2,1,0:T(8,128)}, bf16[64,32,512]{2,1,0:T(8,128)(2,1)S(1)}, ...), condition=%wide.region_3.4_spmd, body=%wide.region_2.3_spmd.sunk | while | flops 274726912 | bytes 34669288 | solution.py:54
  49.6 4.3 copy.17
  58.6 4.3 copy.17
  185.0 10.1 %psum.15 = f32[64]{0:T(128)S(1)} all-reduce(f32[64]{0:T(128)S(1)} %reduce_sum.21), channel_id=1, replica_groups=mesh['dom'=8,'blk'=4] {'blk'}, use_global_device_ids=true, to_apply=%region_6.7 | all-reduce | flops 64 | bytes 512 | tf_op jit(solution)/shard_map/psum | solution.py:58
  195.2 39.9 %all-reduce.2.cloned.1.call-done = f32[16,64,256]{2,1,0:T(8,128)} async-done(((f32[16,64,256]{2,1,0:T(8,128)}), f32[16,64,256]{2,1,0:T(8,128)}) %all-reduce.2.cloned.1.call-update) | async-done | bytes 1048592 | tf_op jit(solution)/shard_map/psum | solution.py:58
  239.5 380.6 %while.30 = (s32[]{:T(128)}, f32[64,32,256]{2,1,0:T(8,128)}, f32[16,64,256]{2,1,0:T(8,128)}, f32[64,8192]{1,0:T(8,128)S(1)}, s32[]{:T(128)}, /*index=5*/s32[]{:T(128)}, s32[]{:T(128)}, s32[]{:T(128)}) while((s32[]{:T(128)}, f32[64,32,256]{2,1,0:T(8,128)}, f32[16,64,256]{2,1,0:T(8,128)}, f32[64,8192]{1,0:T(8,128)S(1)}, ...), condition=%wide.region_10.11_spmd.clone, body=%wide.region_9.10_spmd.clone.sunk | while | flops 1615331328 | bytes 115671328 | solution.py:79
  239.5 7.7 %fusion.24 = f32[256,8192]{1,0:T(8,128)S(1)} fusion(f32[64,8192]{1,0:T(8,128)S(1)} %get-tuple-element.359, f32[16,64,256]{2,1,0:T(8,128)} %get-tuple-element.358, s32[]{:T(128)S(6)} %select_n.83), kind=kOutput, calls=%fused_computation.15.clone.1 | convolution fusion | flops 1610612736 | bytes 10551300 | tf_op jit(solution)/shard_map/while/body/eval_jaxpr/dot_general | solution.py:67
  261.8 7.7 %fusion.24 = f32[256,8192]{1,0:T(8,128)S(1)} fusion(f32[64,8192]{1,0:T(8,128)S(1)} %get-tuple-element.359, f32[16,64,256]{2,1,0:T(8,128)} %get-tuple-element.358, s32[]{:T(128)S(6)} %select_n.83), kind=kOutput, calls=%fused_computation.15.clone.1 | convolution fusion | flops 1610612736 | bytes 10551300 | tf_op jit(solution)/shard_map/while/body/eval_jaxpr/dot_general | solution.py:67
  285.7 7.7 %fusion.24 = f32[256,8192]{1,0:T(8,128)S(1)} fusion(f32[64,8192]{1,0:T(8,128)S(1)} %get-tuple-element.359, f32[16,64,256]{2,1,0:T(8,128)} %get-tuple-element.358, s32[]{:T(128)S(6)} %select_n.83), kind=kOutput, calls=%fused_computation.15.clone.1 | convolution fusion | flops 1610612736 | bytes 10551300 | tf_op jit(solution)/shard_map/while/body/eval_jaxpr/dot_general | solution.py:67
  309.6 7.7 %fusion.24 = f32[256,8192]{1,0:T(8,128)S(1)} fusion(f32[64,8192]{1,0:T(8,128)S(1)} %get-tuple-element.359, f32[16,64,256]{2,1,0:T(8,128)} %get-tuple-element.358, s32[]{:T(128)S(6)} %select_n.83), kind=kOutput, calls=%fused_computation.15.clone.1 | convolution fusion | flops 1610612736 | bytes 10551300 | tf_op jit(solution)/shard_map/while/body/eval_jaxpr/dot_general | solution.py:67
  333.5 7.7 %fusion.24 = f32[256,8192]{1,0:T(8,128)S(1)} fusion(f32[64,8192]{1,0:T(8,128)S(1)} %get-tuple-element.359, f32[16,64,256]{2,1,0:T(8,128)} %get-tuple-element.358, s32[]{:T(128)S(6)} %select_n.83), kind=kOutput, calls=%fused_computation.15.clone.1 | convolution fusion | flops 1610612736 | bytes 10551300 | tf_op jit(solution)/shard_map/while/body/eval_jaxpr/dot_general | solution.py:67
  357.4 7.7 %fusion.24 = f32[256,8192]{1,0:T(8,128)S(1)} fusion(f32[64,8192]{1,0:T(8,128)S(1)} %get-tuple-element.359, f32[16,64,256]{2,1,0:T(8,128)} %get-tuple-element.358, s32[]{:T(128)S(6)} %select_n.83), kind=kOutput, calls=%fused_computation.15.clone.1 | convolution fusion | flops 1610612736 | bytes 10551300 | tf_op jit(solution)/shard_map/while/body/eval_jaxpr/dot_general | solution.py:67
  381.3 7.7 %fusion.24 = f32[256,8192]{1,0:T(8,128)S(1)} fusion(f32[64,8192]{1,0:T(8,128)S(1)} %get-tuple-element.359, f32[16,64,256]{2,1,0:T(8,128)} %get-tuple-element.358, s32[]{:T(128)S(6)} %select_n.83), kind=kOutput, calls=%fused_computation.15.clone.1 | convolution fusion | flops 1610612736 | bytes 10551300 | tf_op jit(solution)/shard_map/while/body/eval_jaxpr/dot_general | solution.py:67
  405.2 7.7 %fusion.24 = f32[256,8192]{1,0:T(8,128)S(1)} fusion(f32[64,8192]{1,0:T(8,128)S(1)} %get-tuple-element.359, f32[16,64,256]{2,1,0:T(8,128)} %get-tuple-element.358, s32[]{:T(128)S(6)} %select_n.83), kind=kOutput, calls=%fused_computation.15.clone.1 | convolution fusion | flops 1610612736 | bytes 10551300 | tf_op jit(solution)/shard_map/while/body/eval_jaxpr/dot_general | solution.py:67
  429.0 7.7 %fusion.24 = f32[256,8192]{1,0:T(8,128)S(1)} fusion(f32[64,8192]{1,0:T(8,128)S(1)} %get-tuple-element.359, f32[16,64,256]{2,1,0:T(8,128)} %get-tuple-element.358, s32[]{:T(128)S(6)} %select_n.83), kind=kOutput, calls=%fused_computation.15.clone.1 | convolution fusion | flops 1610612736 | bytes 10551300 | tf_op jit(solution)/shard_map/while/body/eval_jaxpr/dot_general | solution.py:67
  452.9 7.7 %fusion.24 = f32[256,8192]{1,0:T(8,128)S(1)} fusion(f32[64,8192]{1,0:T(8,128)S(1)} %get-tuple-element.359, f32[16,64,256]{2,1,0:T(8,128)} %get-tuple-element.358, s32[]{:T(128)S(6)} %select_n.83), kind=kOutput, calls=%fused_computation.15.clone.1 | convolution fusion | flops 1610612736 | bytes 10551300 | tf_op jit(solution)/shard_map/while/body/eval_jaxpr/dot_general | solution.py:67
  476.8 7.7 %fusion.24 = f32[256,8192]{1,0:T(8,128)S(1)} fusion(f32[64,8192]{1,0:T(8,128)S(1)} %get-tuple-element.359, f32[16,64,256]{2,1,0:T(8,128)} %get-tuple-element.358, s32[]{:T(128)S(6)} %select_n.83), kind=kOutput, calls=%fused_computation.15.clone.1 | convolution fusion | flops 1610612736 | bytes 10551300 | tf_op jit(solution)/shard_map/while/body/eval_jaxpr/dot_general | solution.py:67
  500.7 7.7 %fusion.24 = f32[256,8192]{1,0:T(8,128)S(1)} fusion(f32[64,8192]{1,0:T(8,128)S(1)} %get-tuple-element.359, f32[16,64,256]{2,1,0:T(8,128)} %get-tuple-element.358, s32[]{:T(128)S(6)} %select_n.83), kind=kOutput, calls=%fused_computation.15.clone.1 | convolution fusion | flops 1610612736 | bytes 10551300 | tf_op jit(solution)/shard_map/while/body/eval_jaxpr/dot_general | solution.py:67
  524.6 7.7 %fusion.24 = f32[256,8192]{1,0:T(8,128)S(1)} fusion(f32[64,8192]{1,0:T(8,128)S(1)} %get-tuple-element.359, f32[16,64,256]{2,1,0:T(8,128)} %get-tuple-element.358, s32[]{:T(128)S(6)} %select_n.83), kind=kOutput, calls=%fused_computation.15.clone.1 | convolution fusion | flops 1610612736 | bytes 10551300 | tf_op jit(solution)/shard_map/while/body/eval_jaxpr/dot_general | solution.py:67
  548.5 7.7 %fusion.24 = f32[256,8192]{1,0:T(8,128)S(1)} fusion(f32[64,8192]{1,0:T(8,128)S(1)} %get-tuple-element.359, f32[16,64,256]{2,1,0:T(8,128)} %get-tuple-element.358, s32[]{:T(128)S(6)} %select_n.83), kind=kOutput, calls=%fused_computation.15.clone.1 | convolution fusion | flops 1610612736 | bytes 10551300 | tf_op jit(solution)/shard_map/while/body/eval_jaxpr/dot_general | solution.py:67
  572.4 7.7 %fusion.24 = f32[256,8192]{1,0:T(8,128)S(1)} fusion(f32[64,8192]{1,0:T(8,128)S(1)} %get-tuple-element.359, f32[16,64,256]{2,1,0:T(8,128)} %get-tuple-element.358, s32[]{:T(128)S(6)} %select_n.83), kind=kOutput, calls=%fused_computation.15.clone.1 | convolution fusion | flops 1610612736 | bytes 10551300 | tf_op jit(solution)/shard_map/while/body/eval_jaxpr/dot_general | solution.py:67
  596.3 7.7 %fusion.24 = f32[256,8192]{1,0:T(8,128)S(1)} fusion(f32[64,8192]{1,0:T(8,128)S(1)} %get-tuple-element.359, f32[16,64,256]{2,1,0:T(8,128)} %get-tuple-element.358, s32[]{:T(128)S(6)} %select_n.83), kind=kOutput, calls=%fused_computation.15.clone.1 | convolution fusion | flops 1610612736 | bytes 10551300 | tf_op jit(solution)/shard_map/while/body/eval_jaxpr/dot_general | solution.py:67
  624.1 35.9 %reduce-scatter.2.cloned.1.call-done = f32[2,4,32,256]{3,2,1,0:T(8,128)} async-done(((f32[16,4,32,256]{3,2,1,0:T(8,128)}), f32[2,4,32,256]{3,2,1,0:T(8,128)}) %reduce-scatter.2.cloned.1.call-update) | async-done | bytes 262160 | tf_op jit(solution)/shard_map/reduce_scatter | solution.py:86
  (532 shorter events, 412.4 us)
Async XLA Ops:
  6.5 28.4 %all-gather.2.cloned.1.call-start = ((), (), s32[]{:S(2)}) async-start(), calls=%async_computation.1 | async-start | bytes 1179648 | tf_op jit(solution)/shard_map/all_gather | solution.py:24
  9.9 225.1 %all-reduce.2.cloned.1.call-start = ((), (), s32[]{:S(2)}) async-start(), calls=%async_computation.2 | async-start | bytes 2097152 | tf_op jit(solution)/shard_map/psum | solution.py:58
  11.5 25.2 %copy-start.12 = (f32[64]{0:T(128)S(1)}, f32[64]{0:T(128)}, u32[]{:S(2)}) copy-start(f32[64]{0:T(128)} %param.12) | copy-start | bytes 772
  94.8 4.3 copy-start.7
  176.3 4.3 copy-start.7
  182.7 477.3 %reduce-scatter.2.cloned.1.call-start = ((), (), s32[]{:S(2)}) async-start(), calls=%async_computation.3 | async-start | bytes 2359296 | tf_op jit(solution)/shard_map/reduce_scatter | solution.py:86
  182.8 52.2 %copy-start.11 = (f32[64]{0:T(128)S(1)}, f32[64]{0:T(128)}, u32[]{:S(2)}) copy-start(f32[64]{0:T(128)} %param.13) | copy-start | bytes 772
  239.5 7.7 %copy-start.5 = (f32[64,8192]{1,0:T(8,128)}, f32[64,8192]{1,0:T(8,128)S(1)}, u32[]{:S(2)}) copy-start(f32[64,8192]{1,0:T(8,128)S(1)} %get-tuple-element.359) | copy-start | bytes 6291460 | tf_op jit(solution)/shard_map/while
  261.8 7.7 %copy-start.5 = (f32[64,8192]{1,0:T(8,128)}, f32[64,8192]{1,0:T(8,128)S(1)}, u32[]{:S(2)}) copy-start(f32[64,8192]{1,0:T(8,128)S(1)} %get-tuple-element.359) | copy-start | bytes 6291460 | tf_op jit(solution)/shard_map/while
  285.7 7.7 %copy-start.5 = (f32[64,8192]{1,0:T(8,128)}, f32[64,8192]{1,0:T(8,128)S(1)}, u32[]{:S(2)}) copy-start(f32[64,8192]{1,0:T(8,128)S(1)} %get-tuple-element.359) | copy-start | bytes 6291460 | tf_op jit(solution)/shard_map/while
  309.6 7.7 %copy-start.5 = (f32[64,8192]{1,0:T(8,128)}, f32[64,8192]{1,0:T(8,128)S(1)}, u32[]{:S(2)}) copy-start(f32[64,8192]{1,0:T(8,128)S(1)} %get-tuple-element.359) | copy-start | bytes 6291460 | tf_op jit(solution)/shard_map/while
  333.5 7.7 %copy-start.5 = (f32[64,8192]{1,0:T(8,128)}, f32[64,8192]{1,0:T(8,128)S(1)}, u32[]{:S(2)}) copy-start(f32[64,8192]{1,0:T(8,128)S(1)} %get-tuple-element.359) | copy-start | bytes 6291460 | tf_op jit(solution)/shard_map/while
  357.4 7.7 %copy-start.5 = (f32[64,8192]{1,0:T(8,128)}, f32[64,8192]{1,0:T(8,128)S(1)}, u32[]{:S(2)}) copy-start(f32[64,8192]{1,0:T(8,128)S(1)} %get-tuple-element.359) | copy-start | bytes 6291460 | tf_op jit(solution)/shard_map/while
  381.3 7.7 %copy-start.5 = (f32[64,8192]{1,0:T(8,128)}, f32[64,8192]{1,0:T(8,128)S(1)}, u32[]{:S(2)}) copy-start(f32[64,8192]{1,0:T(8,128)S(1)} %get-tuple-element.359) | copy-start | bytes 6291460 | tf_op jit(solution)/shard_map/while
  405.1 7.7 %copy-start.5 = (f32[64,8192]{1,0:T(8,128)}, f32[64,8192]{1,0:T(8,128)S(1)}, u32[]{:S(2)}) copy-start(f32[64,8192]{1,0:T(8,128)S(1)} %get-tuple-element.359) | copy-start | bytes 6291460 | tf_op jit(solution)/shard_map/while
  429.0 7.7 %copy-start.5 = (f32[64,8192]{1,0:T(8,128)}, f32[64,8192]{1,0:T(8,128)S(1)}, u32[]{:S(2)}) copy-start(f32[64,8192]{1,0:T(8,128)S(1)} %get-tuple-element.359) | copy-start | bytes 6291460 | tf_op jit(solution)/shard_map/while
  452.9 7.7 %copy-start.5 = (f32[64,8192]{1,0:T(8,128)}, f32[64,8192]{1,0:T(8,128)S(1)}, u32[]{:S(2)}) copy-start(f32[64,8192]{1,0:T(8,128)S(1)} %get-tuple-element.359) | copy-start | bytes 6291460 | tf_op jit(solution)/shard_map/while
  476.8 7.7 %copy-start.5 = (f32[64,8192]{1,0:T(8,128)}, f32[64,8192]{1,0:T(8,128)S(1)}, u32[]{:S(2)}) copy-start(f32[64,8192]{1,0:T(8,128)S(1)} %get-tuple-element.359) | copy-start | bytes 6291460 | tf_op jit(solution)/shard_map/while
  500.7 7.7 %copy-start.5 = (f32[64,8192]{1,0:T(8,128)}, f32[64,8192]{1,0:T(8,128)S(1)}, u32[]{:S(2)}) copy-start(f32[64,8192]{1,0:T(8,128)S(1)} %get-tuple-element.359) | copy-start | bytes 6291460 | tf_op jit(solution)/shard_map/while
  524.6 7.7 %copy-start.5 = (f32[64,8192]{1,0:T(8,128)}, f32[64,8192]{1,0:T(8,128)S(1)}, u32[]{:S(2)}) copy-start(f32[64,8192]{1,0:T(8,128)S(1)} %get-tuple-element.359) | copy-start | bytes 6291460 | tf_op jit(solution)/shard_map/while
  548.5 7.7 %copy-start.5 = (f32[64,8192]{1,0:T(8,128)}, f32[64,8192]{1,0:T(8,128)S(1)}, u32[]{:S(2)}) copy-start(f32[64,8192]{1,0:T(8,128)S(1)} %get-tuple-element.359) | copy-start | bytes 6291460 | tf_op jit(solution)/shard_map/while
  572.4 7.7 %copy-start.5 = (f32[64,8192]{1,0:T(8,128)}, f32[64,8192]{1,0:T(8,128)S(1)}, u32[]{:S(2)}) copy-start(f32[64,8192]{1,0:T(8,128)S(1)} %get-tuple-element.359) | copy-start | bytes 6291460 | tf_op jit(solution)/shard_map/while
  596.3 7.7 %copy-start.5 = (f32[64,8192]{1,0:T(8,128)}, f32[64,8192]{1,0:T(8,128)S(1)}, u32[]{:S(2)}) copy-start(f32[64,8192]{1,0:T(8,128)S(1)} %get-tuple-element.359) | copy-start | bytes 6291460 | tf_op jit(solution)/shard_map/while
  622.4 37.6 %copy-start.1 = (bf16[1,16,4,32,256]{4,3,2,1,0:T(8,128)(2,1)S(1)}, bf16[1,16,4,32,256]{4,3,2,1,0:T(8,128)(2,1)}, u32[]{:S(2)}) copy-start(bf16[1,16,4,32,256]{4,3,2,1,0:T(8,128)(2,1)} %param.10) | copy-start | bytes 3145732
  (82 other events, 175.6 us)
Sparse Core Ops, SparseCore 0:
  10.1 24.7 all-gather.1
  182.8 52.2 all-reduce.1
  624.2 35.7 reduce-scatter.1
where the time goes:
time: 670 us; the launch traced here: 667 us
  local copies, waits for them, and re-layouts  280 us (42%)
  matrix products  156 us (23%)
  other arithmetic  109 us (16%)
  waiting for transfers between devices  96.3 us (14%)
  between operations  13.3 us (2%)
  blocking collectives  10.1 us (2%)
    while x272, local copies, waits for them, and re-layouts  169 us
    dot_general x16, matrix products, accumulate(): lax.dot_general(group_weights, image_float, (((0,), (0,)), ((), ())), pre...  124 us
    slice x80, local copies, waits for them, and re-layouts, accumulate(): running = jnp.roll(running, rot_step, axis=2) + spread[shift_index]  68.4 us
    add x64, other arithmetic, accumulate(): running = jnp.roll(running, rot_step, axis=2) + spread[shift_index]  59.9 us
    psum x1, waiting for transfers between devices, shards(): total_scores, total_norms = lax.psum((scores, norm_part), 'blk')  39.9 us
    reduce_scatter x1, waiting for transfers between devices, shards(): lax.psum_scatter(blocked, 'dom', scatter_dimension=0, tiled=True)  35.9 us
    another operation x16, local copies, waits for them, and re-layouts, correlate(): jnp.stack([window[:, :, shift_index * rot_step:shift_index * rot_step + a...  33.8 us
    dot_general x16, matrix products, correlate(): lax.dot_general(flat_images, rolled, (((1,), (1,)), ((), ())), preferred_...  32.3 us
  transfers between devices with their start and end apart: 3, of which 3 were waited for; matrix products, arithmetic and copies ran while one was open for 1% of the time, Pallas kernels for 0%

commit v1 on v0

v1 whole, which is shorter than its diff:
```python
import functools
import jax
import jax.numpy as jnp
from jax import lax
from jax.experimental import pallas as pl
from jax.experimental.pallas import tpu as pltpu
from jax.sharding import PartitionSpec as P

S = 64
S1 = 8
S2 = 8
G = 4
NT = (((1,), (1,)), ((), ()))


def roll_cycles(x, shift, angles):
    shift = shift % angles
    if shift == 0:
        return x
    parts = [
        pltpu.roll(x[:, c * angles : (c + 1) * angles], shift, 1)
        for c in range(x.shape[1] // angles)
    ]
    return jnp.concatenate(parts, axis=1)


def correlate_kernel(angles, step, img_ref, ref_ref, rolled_ref, score_ref, flat, turned):
    n_dom, _, own, _ = ref_ref.shape
    rows = img_ref.shape[1]
    classes = n_dom * own
    x = img_ref[0].astype(jnp.float32)
    for s1 in range(S1):
        rolled_ref[0, s1 * rows : (s1 + 1) * rows, :] = roll_cycles(
            x, step * s1, angles
        ).astype(jnp.bfloat16)
    for d in range(n_dom):
        flat[d * own : (d + 1) * own, :] = ref_ref[d, 0].astype(jnp.float32)
    y = flat[...]
    half_norm = 0.5 * jnp.sum(y * y, axis=1, keepdims=True)
    for s2 in range(S2):
        turned[s2 * classes : (s2 + 1) * classes, :] = roll_cycles(
            y, -step * S1 * s2, angles
        ).astype(jnp.bfloat16)

    @pl.when(pl.program_id(0) == 0)
    def _():
        score_ref[...] = jnp.zeros_like(score_ref)

    products = lax.dot_general(
        turned[...], rolled_ref[0], NT, preferred_element_type=jnp.float32
    )
    score_ref[...] += products - jnp.tile(half_norm, (S2, 1))


def totals_kernel(angles, step, own, prec_ref, score_ref, rolled_ref, out_ref, high, low):
    rows = score_ref.shape[0]
    classes = rows // S2

    @pl.when(pl.program_id(0) == 0)
    def _():
        logits = score_ref[...] * prec_ref[...]
        top = jnp.max(logits, axis=0, keepdims=True)
        span = top.shape[1] // S1
        top = functools.reduce(
            jnp.maximum, [top[:, i * span : (i + 1) * span] for i in range(S1)]
        )
        e = jnp.exp(logits - jnp.tile(top, (1, S1)))
        mass = jnp.sum(e, axis=0, keepdims=True)
        mass = functools.reduce(
            jnp.add, [mass[:, i * span : (i + 1) * span] for i in range(S1)]
        )
        w = e * jnp.tile(1.0 / mass, (1, S1))
        hi = w.astype(jnp.bfloat16)
        high[...] = hi
        low[...] = (w - hi.astype(jnp.float32)).astype(jnp.bfloat16)

    x = rolled_ref[0]
    spread = jnp.dot(high[...], x, preferred_element_type=jnp.float32)
    spread += jnp.dot(low[...], x, preferred_element_type=jnp.float32)
    running = spread[(S2 - 1) * classes :, :]
    for s2 in reversed(range(S2 - 1)):
        running = (
            roll_cycles(running, step * S1, angles)
            + spread[s2 * classes : (s2 + 1) * classes, :]
        )
    for d in range(classes // own):
        out_ref[d, 0] = running[d * own : (d + 1) * own, :]


def shards(images, ref_store, block_owner, class_gain, precision):
    particles, cycles, angles = images.shape
    n_dom = lax.axis_size("dom")
    blocks = block_owner.shape[0]
    per_block = ref_store.shape[2]
    owned = blocks // n_dom
    own = owned * per_block
    classes = blocks * per_block
    step = angles // S
    groups = cycles // G
    wide = G * angles
    stored = ref_store[0]

    match = block_owner == lax.axis_index("dom")
    ids = jnp.arange(blocks, dtype=jnp.int32)
    rank = jnp.sum(match[None, :] & (ids[None, :] < ids[:, None]), axis=1)
    gains = class_gain.reshape(blocks, per_block)
    picked = []
    for j in range(owned):
        b = jnp.sum(jnp.where(match & (rank == j), ids, 0))
        block = lax.dynamic_index_in_dim(stored, b, 0, keepdims=False)
        gain = lax.dynamic_index_in_dim(gains, b, 0, keepdims=False)
        picked.append(block.astype(jnp.float32) * gain[:, None, None])
    mine = jnp.concatenate(picked, 0).astype(jnp.bfloat16)
    mine = mine.reshape(own, groups, wide).transpose(1, 0, 2)
    refs = lax.all_gather(mine, "dom", axis=0, tiled=False)
    grouped = images.reshape(particles, groups, wide).transpose(1, 0, 2)

    lhs = S2 * classes
    rhs = S1 * particles
    rolled, scores = pl.pallas_call(
        functools.partial(correlate_kernel, angles, step),
        grid=(groups,),
        in_specs=[
            pl.BlockSpec((1, particles, wide), lambda g: (g, 0, 0)),
            pl.BlockSpec((n_dom, 1, own, wide), lambda g: (0, g, 0, 0)),
        ],
        out_specs=[
            pl.BlockSpec((1, rhs, wide), lambda g: (g, 0, 0)),
            pl.BlockSpec((lhs, rhs), lambda g: (0, 0)),
        ],
        out_shape=[
            jax.ShapeDtypeStruct((groups, rhs, wide), jnp.bfloat16),
            jax.ShapeDtypeStruct((lhs, rhs), jnp.float32),
        ],
        scratch_shapes=[
            pltpu.VMEM((classes, wide), jnp.float32),
            pltpu.VMEM((lhs, wide), jnp.bfloat16),
        ],
        compiler_params=pltpu.CompilerParams(vmem_limit_bytes=48 * 1024 * 1024),
        name="correlate",
    )(grouped, refs)
    scores = lax.psum(scores, "blk")
    prec = jnp.tile(precision, S1)[None, :]
    parts = pl.pallas_call(
        functools.partial(totals_kernel, angles, step, own),
        grid=(groups,),
        in_specs=[
            pl.BlockSpec((1, rhs), lambda g: (0, 0)),
            pl.BlockSpec((lhs, rhs), lambda g: (0, 0)),
            pl.BlockSpec((1, rhs, wide), lambda g: (g, 0, 0)),
        ],
        out_specs=pl.BlockSpec((n_dom, 1, own, wide), lambda g: (0, g, 0, 0)),
        out_shape=jax.ShapeDtypeStruct((n_dom, groups, own, wide), jnp.float32),
        scratch_shapes=[
            pltpu.VMEM((lhs, rhs), jnp.bfloat16),
            pltpu.VMEM((lhs, rhs), jnp.bfloat16),
        ],
        compiler_params=pltpu.CompilerParams(vmem_limit_bytes=48 * 1024 * 1024),
        name="totals",
    )(prec, scores, rolled)
    mine_sum = lax.psum_scatter(parts, "dom", scatter_dimension=0, tiled=True)[0]
    mine_sum = mine_sum.transpose(1, 0, 2).reshape(owned, per_block, cycles, angles)
    return mine_sum[None]


def solution(mesh):
    return jax.shard_map(
        shards,
        mesh=mesh,
        in_specs=(P("dom", "blk", None), P("dom", None, None, "blk", None), P(), P(), P("dom")),
        out_specs=P("dom", None, None, "blk", None),
        check_vma=False,
    )
```

time: 670 us -> 168 us (0.25)
  local copies, waits for them, and re-layouts: 280 us -> 8.25 us
  matrix products: 156 us -> 0 us
  other arithmetic: 109 us -> 3.15 us
  Pallas kernels: 0 us -> 28.4 us
  waiting for transfers between devices: 96.3 us -> 111 us
  blocking collectives: 10.1 us -> 0 us
    while x272 -> x0, local copies, waits for them, and re-layouts: 169 us -> none
    dot_general x32 -> x0, matrix products: 156 us -> none  [the longest x16 124 us: accumulate(): lax.dot_general(group_weights, image_float, (((0,), (0,)), ((), ())), pre...]
    slice x80 -> x0, local copies, waits for them, and re-layouts: 68.4 us -> none  [accumulate(): running = jnp.roll(running, rot_step, axis=2) + spread[shift_index]]
    add x64 -> x0, other arithmetic: 59.9 us -> none  [accumulate(): running = jnp.roll(running, rot_step, axis=2) + spread[shift_index]]
    another operation x17 -> x3, local copies, waits for them, and re-layouts: 33.8 us -> 0.86 us  [the longest x1 0.78 us: shards(): return mine_sum[None]]
    pallas_call x0 -> x2, Pallas kernels: none -> 28.4 us  [the longest x1 17.2 us: shards(): pl.pallas_call(functools.partial(totals_kernel, angles, step, own), grid=...]
    while x16 -> x0, other arithmetic: 26.7 us -> none
    psum x1, waiting for transfers between devices: 39.9 us -> 52.2 us  [shards(): scores = lax.psum(scores, 'blk')]
where the time goes in v1:
time: 168 us
  waiting for transfers between devices  111 us (66%)
  Pallas kernels  28.4 us (17%)
  between operations  17 us (10%)
  local copies, waits for them, and re-layouts  8.25 us (5%)
  other arithmetic  3.15 us (2%)
    psum x1, waiting for transfers between devices, shards(): scores = lax.psum(scores, 'blk')  52.2 us
    reduce_scatter x1, waiting for transfers between devices, shards(): lax.psum_scatter(parts, 'dom', scatter_dimension=0, tiled=True)[0]  35.9 us
    all_gather x1, waiting for transfers between devices, shards(): refs = lax.all_gather(mine, 'dom', axis=0, tiled=False)  22.6 us
    pallas_call x1, Pallas kernels, shards(): pl.pallas_call(functools.partial(totals_kernel, angles, step, own), grid=...  17.2 us
    pallas_call x1, Pallas kernels, shards(): pl.pallas_call(functools.partial(correlate_kernel, angles, step), grid=(g...  11.1 us
  transfers between devices with their start and end apart: 3, of which 3 were waited for; matrix products, arithmetic and copies ran while one was open for 1% of the time, Pallas kernels for 0%

profile of v1, /device:TPU:0, one launch (start us, length us, event | category | flops | bytes accessed | tf_op | source)
XLA Modules:
  0.0 167.7 jit_solution(4010915561054131200)
XLA Ops:
  6.5 0.7 broadcast_compare_fusion
  7.2 0.1 convert_reduce_fusion
  7.3 1.4 fusion.3
  12.5 0.9 dynamic-slice_convert_fusion.1
  13.5 0.7 reshape.26
  14.3 0.1 multiply_convert_fusion
  14.4 0.7 copy.18
  15.1 0.0 all-gather.3.cloned.1.call-update
  15.2 0.0 all-reduce.2.cloned.1.call-start
  15.2 1.7 %reshape.25 = bf16[64,8,1024]{2,1,0:T(8,128)(2,1)S(1)} reshape(bf16[64,32,256]{2,1,0:T(8,128)(2,1)} %param.5) | data formatting | bytes 2097152 | tf_op jit(solution)/shard_map/reshape | solution.py:116
  16.9 0.6 copy.21
  17.5 22.6 %all-gather.3.cloned.1.call-done = bf16[64,8,1024]{2,1,0:T(8,128)(2,1)} async-done(((bf16[8,8,1024]{2,1,0:T(8,128)(2,1)}), bf16[64,8,1024]{2,1,0:T(8,128)(2,1)}) %all-gather.3.cloned.1.call-update) | async-done | bytes 1048592 | tf_op jit(solution)/shard_map/all_gather | solution.py:115
  40.1 1.2 copy-done.1
  41.3 11.1 %correlate.1 = (bf16[8,512,1024]{2,1,0:T(8,128)(2,1)}, f32[512,512]{1,0:T(8,128)}) custom-call(bf16[8,64,1024]{2,1,0:T(8,128)(2,1)S(1)} %bitcast.17, bf16[8,8,8,1024]{3,2,1,0:T(8,128)(2,1)S(1)} %bitcast.18), custom_call_target="tpu_custom_call" | custom-call | tf_op jit(solution)/shard_map/correlate/pallas_call | solution.py:120
  52.5 0.0 all-reduce.2.cloned.1.call-update
  52.5 0.0 reduce-scatter.2.cloned.1.call-start
  52.6 0.1 broadcast_in_dim_tile.3.prec_ref
  52.6 52.2 %all-reduce.2.cloned.1.call-done.score_ref = f32[512,512]{1,0:T(8,128)} async-done(((f32[512,512]{1,0:T(8,128)}), f32[512,512]{1,0:T(8,128)}) %all-reduce.2.cloned.1.call-update) | async-done | bytes 1048592 | tf_op jit(solution)/shard_map/psum | solution.py:142
  104.8 1.2 copy-done
  106.1 17.2 %totals.1 = f32[8,8,8,1024]{3,2,1,0:T(8,128)} custom-call(f32[1,512]{1,0:T(1,128)S(1)} %broadcast_in_dim_tile.3.prec_ref, f32[512,512]{1,0:T(8,128)S(1)} %copy-done, bf16[8,512,1024]{2,1,0:T(8,128)(2,1)} %get-tuple-element.8.rolled_ref), custom_call_target="tpu_custom_call" | custom-call | tf_op jit(solution)/shard_map/totals/pallas_call | solution.py:144
  123.3 0.0 reduce-scatter.2.cloned.1.call-update
  123.3 35.9 %reduce-scatter.2.cloned.1.call-done = f32[1,8,8,1024]{3,2,1,0:T(8,128)} async-done(((f32[8,8,8,1024]{3,2,1,0:T(8,128)}), f32[1,8,8,1024]{3,2,1,0:T(8,128)}) %reduce-scatter.2.cloned.1.call-update) | async-done | bytes 262160 | tf_op jit(solution)/shard_map/reduce_scatter | solution.py:161
  159.2 1.1 copy.19
  160.3 0.8 broadcast_in_dim_reshape.3
  (10 shorter events, 0.1 us)
Async XLA Ops:
  6.5 46.0 %copy-start.2 = (f32[64]{0:T(128)S(1)}, f32[64]{0:T(128)}, u32[]{:S(2)}) copy-start(f32[64]{0:T(128)} %param.9) | copy-start | bytes 772
  6.5 33.6 %all-gather.3.cloned.1.call-start = ((), (), s32[]{:S(2)}) async-start(), calls=%async_computation.3 | async-start | bytes 1179648 | tf_op jit(solution)/shard_map/all_gather | solution.py:115
  15.2 89.7 %all-reduce.2.cloned.1.call-start = ((), (), s32[]{:S(2)}) async-start(), calls=%async_computation.1 | async-start | bytes 2097152 | tf_op jit(solution)/shard_map/psum | solution.py:142
  40.1 1.2 copy-start.1
  52.5 106.7 %reduce-scatter.2.cloned.1.call-start = ((), (), s32[]{:S(2)}) async-start(), calls=%async_computation.2 | async-start | bytes 2359296 | tf_op jit(solution)/shard_map/reduce_scatter | solution.py:161
  104.8 1.2 copy-start
Sparse Core Ops, SparseCore 0:
  15.3 24.7 all-gather.2
  52.6 52.1 all-reduce.1
  123.5 35.7 reduce-scatter.1

commit v2 on v0

v2 whole, which is shorter than its diff:
```python
import functools
import jax
import jax.numpy as jnp
from jax import lax
from jax.experimental import pallas as pl
from jax.experimental.pallas import tpu as pltpu
from jax.sharding import PartitionSpec as P

S = 64
S1 = 8
S2 = 8
G = 4
UNIT = 16
PIECES = 4
NT = (((1,), (1,)), ((), ()))
MESH = pl.DeviceIdType.MESH


def roll_cycles(x, shift, angles):
    shift = shift % angles
    if shift == 0:
        return x
    parts = [
        pltpu.roll(x[:, c * angles : (c + 1) * angles], shift, 1)
        for c in range(x.shape[1] // angles)
    ]
    return jnp.concatenate(parts, axis=1)


def spread_lanes(op, x, width):
    shift = width
    while shift < x.shape[1]:
        x = op(x, pltpu.roll(x, shift, 1))
        shift *= 2
    return x


def kernel(
    n_dom, n_blk, angles, per_block, owned,
    owner_ref, gain_ref, prec_ref, img_ref, store_ref, out_ref,
    minef, refs, rolled, turned, flat, norm, scores, got, weights, parts, sib, zout, zin,
    ref_send, ref_recv, fwd_send, score_send, score_recv, w_send, w_recv,
    sib_send, sib_recv, z_send, z_recv,
):
    step = angles // S
    own = owned * per_block
    chips = n_dom // 2
    unit_devs = UNIT // own
    units = n_dom // unit_devs
    groups, particles, wide = img_ref.shape
    pp = particles // n_blk
    blocks = store_ref.shape[0]
    me = lax.axis_index("dom")
    blk = lax.axis_index("blk")
    chip = me // 2
    core = me % 2
    sibling = chip * 2 + 1 - core
    far = [lax.rem(chip + o, chips) for o in range(1, chips)]
    pair = blk // 2
    blk_peers = [(1 - pair) * 2, (1 - pair) * 2 + 1, pair * 2 + 1 - blk % 2]

    barrier = pltpu.get_barrier_semaphore()
    for c in far:
        pl.semaphore_signal(barrier, inc=1, device_id={"dom": c * 2 + core}, device_id_type=MESH)
    pl.semaphore_signal(barrier, inc=1, device_id={"dom": sibling}, device_id_type=MESH)
    for b in blk_peers:
        pl.semaphore_signal(barrier, inc=1, device_id={"blk": b}, device_id_type=MESH)

    picks = [jnp.int32(0)] * owned
    seen = jnp.int32(0)
    for b in range(blocks):
        hit = (owner_ref[b] == me).astype(jnp.int32)
        for j in range(owned):
            take = jnp.logical_and(hit == 1, seen == j)
            picks[j] = jnp.where(take, jnp.int32(b), picks[j])
        seen = seen + hit
    for j in range(owned):
        block = store_ref[picks[j]].astype(jnp.float32)
        row = lax.broadcasted_iota(jnp.int32, block.shape, 0) & (per_block - 1)
        gain = jnp.zeros_like(block)
        for i in range(per_block):
            gain = jnp.where(row == i, gain_ref[picks[j] * per_block + i], gain)
        block = block * gain
        for g in range(groups):
            at = (g % 2) * own + j * per_block
            minef[g // 2, at : at + per_block, :] = block[g * per_block : (g + 1) * per_block, :]
    refs[me] = minef[...].astype(jnp.bfloat16)

    pl.semaphore_wait(barrier, len(far) + 1 + len(blk_peers))

    def ref_copy(slot, target, send):
        return pltpu.make_async_remote_copy(
            src_ref=refs.at[slot], dst_ref=refs.at[slot], send_sem=send,
            recv_sem=ref_recv.at[slot], device_id={"dom": target}, device_id_type=MESH,
        )

    out_copies = [ref_copy(me, c * 2 + core, ref_send.at[o]) for o, c in enumerate(far)]
    out_copies.append(ref_copy(me, sibling, ref_send.at[chips - 1]))
    for copy in out_copies:
        copy.start()

    def roll_images(g, carry):
        x = img_ref[g].astype(jnp.float32)
        for s1 in range(S1):
            r = roll_cycles(x, step * s1, angles).astype(jnp.bfloat16)
            for j in range(n_blk):
                at = j * pp * S1 + s1 * pp
                rolled[g, at : at + pp, :] = r[j * pp : (j + 1) * pp, :]
        return carry

    lax.fori_loop(0, groups, roll_images, 0)
    norm[...] = jnp.zeros_like(norm)

    fwd = []
    for o, c in enumerate(far):
        slot = c * 2 + core
        ref_copy(slot, slot, ref_send.at[o]).wait_recv()
        copy = ref_copy(slot, sibling, fwd_send.at[o])
        copy.start()
        fwd.append(copy)
    ref_copy(sibling, sibling, ref_send.at[chips - 1]).wait_recv()
    for o, c in enumerate(far):
        slot = c * 2 + 1 - core
        ref_copy(slot, sibling, fwd_send.at[o]).wait_recv()

    def turn_refs(gp, carry):
        for u in range(units):
            for e in range(unit_devs):
                y = refs[u * unit_devs + e, gp].astype(jnp.float32)
                for h in range(2):
                    flat[u, h, e * own : (e + 1) * own, :] = y[h * own : (h + 1) * own, :]
            for h in range(2):
                y = flat[u, h]
                half = 0.5 * jnp.sum(y * y, axis=1, keepdims=True)
                norm[u] += jnp.broadcast_to(half, (UNIT, norm.shape[2]))
                for s2 in range(S2):
                    at = u * S2 * UNIT + s2 * UNIT
                    turned[gp * 2 + h, at : at + UNIT, :] = roll_cycles(
                        y, -step * S1 * s2, angles
                    ).astype(jnp.bfloat16)
        return carry

    lax.fori_loop(0, groups // 2, turn_refs, 0)

    lanes = pp * S1

    def score_pair(which):
        first = which * 2
        for i in range(2):
            for u in range(units):
                for s2 in range(S2):
                    at = u * S2 * UNIT + s2 * UNIT
                    scores[first + i, at : at + UNIT, :] = -norm[u]

        def body(g, carry):
            cols = rolled[g, pl.ds(pl.multiple_of(which * 2 * lanes, 2 * lanes), 2 * lanes), :]
            prod = lax.dot_general(turned[g], cols, NT, preferred_element_type=jnp.float32)
            for i in range(2):
                scores[first + i] += prod[:, i * lanes : (i + 1) * lanes]
            return carry

        lax.fori_loop(0, groups, body, 0)

    def score_copy(src, slot, target, o):
        return pltpu.make_async_remote_copy(
            src_ref=scores.at[src], dst_ref=got.at[slot], send_sem=score_send.at[o],
            recv_sem=score_recv.at[slot], device_id={"blk": target}, device_id_type=MESH,
        )

    score_copies = [score_copy(b, blk, b, o) for o, b in enumerate(blk_peers)]
    score_pair(1 - pair)
    score_copies[1].start()
    score_copies[0].start()
    score_pair(pair)
    score_copies[2].start()
    for o in (2, 0, 1):
        b = blk_peers[o]
        score_copy(b, b, b, o).wait_recv()
    total = scores[blk]
    for b in blk_peers:
        total = total + got[b]
    logits = total * prec_ref[blk][0:1, :]
    top = jnp.broadcast_to(jnp.max(logits, axis=0, keepdims=True), (8, lanes))
    top = spread_lanes(jnp.maximum, top, pp)[0:1, :]
    e = jnp.exp(logits - top)
    mass = jnp.broadcast_to(jnp.sum(e, axis=0, keepdims=True), (8, lanes))
    mass = spread_lanes(jnp.add, mass, pp)[0:1, :]
    weights[blk] = (e * (1.0 / mass)).astype(jnp.bfloat16)

    def w_copy(slot, target, o):
        return pltpu.make_async_remote_copy(
            src_ref=weights.at[slot], dst_ref=weights.at[slot], send_sem=w_send.at[o],
            recv_sem=w_recv.at[slot], device_id={"blk": target}, device_id_type=MESH,
        )

    w_copies = [w_copy(blk, b, o) for o, b in enumerate(blk_peers)]
    for o in (1, 0, 2):
        w_copies[o].start()
    for o, b in enumerate(blk_peers):
        w_copy(b, b, o).wait_recv()

    per_piece = groups // PIECES

    def sib_copy(q, which):
        return pltpu.make_async_remote_copy(
            src_ref=parts.at[which, q], dst_ref=sib.at[q], send_sem=sib_send.at[q],
            recv_sem=sib_recv.at[q], device_id={"dom": sibling}, device_id_type=MESH,
        )

    def z_copy(q, src, slot, target, o):
        return pltpu.make_async_remote_copy(
            src_ref=zout.at[q, src], dst_ref=zin.at[q, slot], send_sem=z_send.at[q, o],
            recv_sem=z_recv.at[q, slot], device_id={"dom": target * 2 + core}, device_id_type=MESH,
        )

    sib_copies, z_copies = [], []
    for q in range(PIECES + 1):
        if q < PIECES:

            def body(gi, carry, q=q):
                w = jnp.concatenate([weights[j] for j in range(n_blk)], axis=1)
                spread = jnp.dot(
                    w, rolled[q * per_piece + gi], preferred_element_type=jnp.float32
                )
                for u in range(units):
                    base = u * S2 * UNIT
                    running = spread[base + (S2 - 1) * UNIT : base + S2 * UNIT, :]
                    for s2 in reversed(range(S2 - 1)):
                        running = (
                            roll_cycles(running, step * S1, angles)
                            + spread[base + s2 * UNIT : base + (s2 + 1) * UNIT, :]
                        )
                    for k in range(unit_devs):
                        d = u * unit_devs + k
                        parts[d % 2, q, d // 2, gi] = running[k * own : (k + 1) * own, :]
                return carry

            lax.fori_loop(0, per_piece, body, 0)
            copy = sib_copy(q, 1 - core)
            copy.start()
            sib_copies.append(copy)
        if q >= 1:
            p = q - 1
            sib_copy(p, 1 - core).wait_recv()
            for c in range(chips):
                both = parts[core, p, c] + sib[p, c]
                parts[core, p, c] = both
                zout[p, c] = both.reshape(per_piece * own, wide).astype(jnp.bfloat16)
            for o, c in enumerate(far):
                copy = z_copy(p, c, chip, c, o)
                copy.start()
                z_copies.append(copy)

    for q in range(PIECES):
        total = parts[core, q, chip].reshape(per_piece * own, wide)
        for o, c in enumerate(far):
            z_copy(q, c, c, c, o).wait_recv()
            total = total + zin[q, c].astype(jnp.float32)
        for gi in range(per_piece):
            for rr in range(G):
                out_ref[:, (q * per_piece + gi) * G + rr, :] = total[
                    gi * own : (gi + 1) * own, rr * angles : (rr + 1) * angles
                ]

    for copy in out_copies + fwd + score_copies + w_copies + sib_copies + z_copies:
        copy.wait_send()


def shards(images, ref_store, block_owner, class_gain, precision):
    particles, cycles, angles = images.shape
    n_dom = lax.axis_size("dom")
    n_blk = lax.axis_size("blk")
    blocks = block_owner.shape[0]
    per_block = ref_store.shape[2]
    owned = blocks // n_dom
    own = owned * per_block
    classes = blocks * per_block
    groups = cycles // G
    wide = G * angles
    chips = n_dom // 2
    units = classes // UNIT
    pp = particles // n_blk
    lhs = S2 * classes
    rhs = S1 * particles
    per_piece = groups // PIECES

    grouped = images.reshape(particles, groups, wide).transpose(1, 0, 2)
    store = ref_store[0].reshape(blocks, per_block, groups, wide).transpose(0, 2, 1, 3)
    store = store.reshape(blocks, groups * per_block, wide)
    prec = jnp.tile(precision.reshape(n_blk, 1, pp), (1, 8, S1))

    vmem = pl.BlockSpec(memory_space=pltpu.VMEM)
    smem = pl.BlockSpec(memory_space=pltpu.SMEM)
    bf16, f32 = jnp.bfloat16, jnp.float32
    dma = pltpu.SemaphoreType.DMA
    out = pl.pallas_call(
        functools.partial(kernel, n_dom, n_blk, angles, per_block, owned),
        in_specs=[smem, smem, vmem, vmem, vmem],
        out_specs=vmem,
        out_shape=jax.ShapeDtypeStruct((own, cycles, angles), f32),
        scratch_shapes=[
            pltpu.VMEM((groups // 2, 2 * own, wide), f32),
            pltpu.VMEM((n_dom, groups // 2, 2 * own, wide), bf16),
            pltpu.VMEM((groups, rhs, wide), bf16),
            pltpu.VMEM((groups, lhs, wide), bf16),
            pltpu.VMEM((units, 2, UNIT, wide), f32),
            pltpu.VMEM((units, UNIT, pp * S1), f32),
            pltpu.VMEM((n_blk, lhs, pp * S1), f32),
            pltpu.VMEM((n_blk, lhs, pp * S1), f32),
            pltpu.VMEM((n_blk, lhs, pp * S1), bf16),
            pltpu.VMEM((2, PIECES, chips, per_piece, own, wide), f32),
            pltpu.VMEM((PIECES, chips, per_piece, own, wide), f32),
            pltpu.VMEM((PIECES, chips, per_piece * own, wide), bf16),
            pltpu.VMEM((PIECES, chips, per_piece * own, wide), bf16),
            dma((chips,)), dma((n_dom,)), dma((chips,)),
            dma((n_blk,)), dma((n_blk,)), dma((n_blk,)), dma((n_blk,)),
            dma((PIECES,)), dma((PIECES,)), dma((PIECES, chips)), dma((PIECES, chips)),
        ],
        compiler_params=pltpu.CompilerParams(
            collective_id=0, has_side_effects=True, vmem_limit_bytes=52 * 1024 * 1024
        ),
        cost_estimate=pl.CostEstimate(
            flops=4 * lhs * rhs * groups * wide, bytes_accessed=4 * 1024 * 1024, transcendentals=0
        ),
        name="fused",
    )(block_owner, class_gain, prec, grouped, store)
    return out.reshape(1, owned, per_block, cycles, angles)


def solution(mesh):
    return jax.shard_map(
        shards,
        mesh=mesh,
        in_specs=(P("dom", "blk", None), P("dom", None, None, "blk", None), P(), P(), P("dom")),
        out_specs=P("dom", None, None, "blk", None),
        check_vma=False,
    )
```

time: 670 us -> 73.1 us (0.11)
  local copies, waits for them, and re-layouts: 280 us -> 7.6 us
  matrix products: 156 us -> 0 us
  other arithmetic: 109 us -> 0 us
  waiting for transfers between devices: 96.3 us -> 0 us
  Pallas kernels: 0 us -> 65.2 us
  between operations: 13.3 us -> 0.07 us
  blocking collectives: 10.1 us -> 0 us
    while x272 -> x0, local copies, waits for them, and re-layouts: 169 us -> none
    dot_general x32 -> x0, matrix products: 156 us -> none  [the longest x16 124 us: accumulate(): lax.dot_general(group_weights, image_float, (((0,), (0,)), ((), ())), pre...]
    slice x80 -> x0, local copies, waits for them, and re-layouts: 68.4 us -> none  [accumulate(): running = jnp.roll(running, rot_step, axis=2) + spread[shift_index]]
    pallas_call x0 -> x1, Pallas kernels: none -> 65.2 us  [shards(): pl.pallas_call(functools.partial(kernel, n_dom, n_blk, angles, per_block,...]
    add x64 -> x0, other arithmetic: 59.9 us -> none  [accumulate(): running = jnp.roll(running, rot_step, axis=2) + spread[shift_index]]
    psum x1 -> x0, waiting for transfers between devices: 39.9 us -> none  [shards(): total_scores, total_norms = lax.psum((scores, norm_part), 'blk')]
    reduce_scatter x1 -> x0, waiting for transfers between devices: 35.9 us -> none  [shards(): lax.psum_scatter(blocked, 'dom', scatter_dimension=0, tiled=True)]
    another operation x17 -> x6, local copies, waits for them, and re-layouts: 33.8 us -> 2.76 us  [the longest x2 2.59 us: shards(): ref_store[0].reshape(blocks, per_block, groups, wide).transpose(0, 2, 1, 3)]
  transfers between devices with their start and end apart: 3 -> 0, of which waited for: 3 -> 0; matrix products, arithmetic and copies ran while one was open for 1% -> 0% of each run, Pallas kernels for 0% -> 0%
where the time goes in v2:
time: 73.1 us; the launch traced here: 72.8 us
  Pallas kernels  65.2 us (89%)
  local copies, waits for them, and re-layouts  7.6 us (10%)
    pallas_call x1, Pallas kernels, shards(): pl.pallas_call(functools.partial(kernel, n_dom, n_blk, angles, per_block,...  65.2 us
    another operation x2, local copies, waits for them, and re-layouts, shards(): ref_store[0].reshape(blocks, per_block, groups, wide).transpose(0, 2, 1, 3)  2.59 us
    unnamed x9, local copies, waits for them, and re-layouts  2.5 us

profile of v2, /device:TPU:0, one launch (start us, length us, event | category | flops | bytes accessed | tf_op | source)
XLA Modules:
  0.0 72.8 jit_solution(15064099743121139863)
XLA Ops:
  0.0 1.7 %reshape_squeeze.3 = bf16[16,4,8,1024]{3,2,1,0:T(8,128)(2,1)S(1)} reshape(bf16[1,16,4,32,256]{4,3,2,1,0:T(8,128)(2,1)} %param.6) | data formatting | bytes 2097152 | tf_op jit(solution)/shard_map/reshape;squeeze | solution.py:288
  1.7 0.9 %copy.11 = bf16[16,4,8,1024]{3,1,2,0:T(4,128)(2,1)S(1)} copy(bf16[16,4,8,1024]{3,2,1,0:T(8,128)(2,1)S(1)} %reshape_squeeze.3) | data formatting | bytes 2097152 | tf_op jit(solution)/shard_map/reshape;squeeze | solution.py:288
  2.6 0.0 copy-start.2
  2.6 1.1 %reshape.14.store_ref = bf16[16,32,1024]{2,1,0:T(8,128)(2,1)} reshape(bf16[16,8,4,1024]{3,2,1,0:T(4,128)(2,1)S(1)} %bitcast.11) | data formatting | bytes 2097152 | tf_op jit(solution)/shard_map/reshape | solution.py:289
  3.7 0.5 copy-done.2
  4.2 0.7 reshape.13
  4.9 0.6 copy.12
  5.5 0.0 copy-start.3
  5.5 0.6 copy-done.3
  6.1 0.1 tile.12
  6.2 0.1 tile.14
  6.3 0.0 copy-start
  6.3 0.0 copy-start.1
  6.3 0.6 copy-done
  6.9 0.0 copy-done.1
  7.0 65.2 %fused.1 = f32[8,32,256]{2,1,0:T(8,128)S(1)} custom-call(s32[16]{0:T(128)S(1)} %copy-done, f32[64]{0:T(128)S(1)} %copy-done.1, f32[4,8,128]{2,1,0:T(8,128)S(1)} %tile.15.prec_ref, bf16[8,64,1024]{2,1,0:T(8,128)(2,1)S(1)} %bitcast.9, bf16[16,32,1024]{2,1,0:T(8,128)(2,1)} %reshape.14.store_ref), custom_call_target="tpu_custom_call" | custom-call | flops 8589934592 | bytes 4194304 | tf_op jit(solution)/shard_map/fused/pallas_call | solution.py:296
  72.1 0.7 copy.14
  (2 shorter events, 0.0 us)
Async XLA Ops:
  2.6 1.6 %copy-start.2 = (bf16[64,32,256]{2,1,0:T(8,128)(2,1)S(1)}, bf16[64,32,256]{2,1,0:T(8,128)(2,1)}, u32[]{:S(2)}) copy-start(bf16[64,32,256]{2,1,0:T(8,128)(2,1)} %param.5) | copy-start | bytes 3145732
  5.5 0.7 copy-start.3
  6.3 0.7 copy-start
  6.3 0.7 copy-start.1

commit v3 on v2

--- a/solution.py
+++ b/solution.py
@@ -10,8 +10,8 @@
 S1 = 8
 S2 = 8
 G = 4
-UNIT = 16
 PIECES = 4
+LANES = 128
 NT = (((1,), (1,)), ((), ()))
 MESH = pl.DeviceIdType.MESH
 
@@ -27,6 +27,12 @@
     return jnp.concatenate(parts, axis=1)
 
 
+def every(ref, start, count, stride):
+    return jnp.concatenate(
+        [ref[h, pl.ds(start, count, stride=stride), :] for h in range(ref.shape[0])], axis=1
+    )
+
+
 def spread_lanes(op, x, width):
     shift = width
     while shift < x.shape[1]:
@@ -38,16 +44,20 @@
 def kernel(
     n_dom, n_blk, angles, per_block, owned,
     owner_ref, gain_ref, prec_ref, img_ref, store_ref, out_ref,
-    minef, refs, rolled, turned, flat, norm, scores, got, weights, parts, sib, zout, zin,
+    imgf, blockf, minef, refs, rolled, turned, flat, norm, scores, got, weights, parts, sib, zout, zin,
     ref_send, ref_recv, fwd_send, score_send, score_recv, w_send, w_recv,
     sib_send, sib_recv, z_send, z_recv,
 ):
     step = angles // S
     own = owned * per_block
     chips = n_dom // 2
-    unit_devs = UNIT // own
-    units = n_dom // unit_devs
-    groups, particles, wide = img_ref.shape
+    unit = 2 * own
+    span = S2 * unit
+    groups = rolled.shape[0]
+    cycles = groups * G
+    particles = img_ref.shape[0] // cycles
+    wide = G * angles
+    halves = angles // LANES
     pp = particles // n_blk
     blocks = store_ref.shape[0]
     me = lax.axis_index("dom")
@@ -76,14 +86,18 @@
         seen = seen + hit
     for j in range(owned):
         block = store_ref[picks[j]].astype(jnp.float32)
-        row = lax.broadcasted_iota(jnp.int32, block.shape, 0) & (per_block - 1)
-        gain = jnp.zeros_like(block)
         for i in range(per_block):
-            gain = jnp.where(row == i, gain_ref[picks[j] * per_block + i], gain)
-        block = block * gain
-        for g in range(groups):
-            at = (g % 2) * own + j * per_block
-            minef[g // 2, at : at + per_block, :] = block[g * per_block : (g + 1) * per_block, :]
+            k = j * per_block + i
+            gain = gain_ref[picks[j] * per_block + i]
+            for h in range(halves):
+                blockf[h, k * cycles : (k + 1) * cycles, :] = (
+                    block[i * cycles : (i + 1) * cycles, h * LANES : (h + 1) * LANES] * gain
+                )
+    for r in range(cycles):
+        g, rr = r // G, r % G
+        minef[g // 2, (g % 2) * own : (g % 2 + 1) * own, rr * angles : (rr + 1) * angles] = (
+            every(blockf, r, own, cycles)
+        )
     refs[me] = minef[...].astype(jnp.bfloat16)
 
     pl.semaphore_wait(barrier, len(far) + 1 + len(blk_peers))
@@ -99,86 +113,90 @@
     for copy in out_copies:
         copy.start()
 
+    def widen(i, carry):
+        at = pl.ds(pl.multiple_of(i * 256, 256), 256)
+        for h in range(halves):
+            imgf[h, at, :] = img_ref[at, h * LANES : (h + 1) * LANES].astype(jnp.float32)
+        return carry
+
+    lax.fori_loop(0, particles * cycles // 256, widen, 0)
+
     def roll_images(g, carry):
-        x = img_ref[g].astype(jnp.float32)
-        for s1 in range(S1):
-            r = roll_cycles(x, step * s1, angles).astype(jnp.bfloat16)
-            for j in range(n_blk):
-                at = j * pp * S1 + s1 * pp
-                rolled[g, at : at + pp, :] = r[j * pp : (j + 1) * pp, :]
+        for rr in range(G):
+            x = every(imgf, g * G + rr, particles, cycles)
+            for s1 in range(S1):
+                r = roll_cycles(x, step * s1, angles).astype(jnp.bfloat16)
+                for j in range(n_blk):
+                    at = j * pp * S1 + s1 * pp
+                    rolled[g, at : at + pp, rr * angles : (rr + 1) * angles] = r[
+                        j * pp : (j + 1) * pp, :
+                    ]
         return carry
 
     lax.fori_loop(0, groups, roll_images, 0)
-    norm[...] = jnp.zeros_like(norm)
-
-    fwd = []
-    for o, c in enumerate(far):
-        slot = c * 2 + core
-        ref_copy(slot, slot, ref_send.at[o]).wait_recv()
-        copy = ref_copy(slot, sibling, fwd_send.at[o])
-        copy.start()
-        fwd.append(copy)
-    ref_copy(sibling, sibling, ref_send.at[chips - 1]).wait_recv()
-    for o, c in enumerate(far):
-        slot = c * 2 + 1 - core
-        ref_copy(slot, sibling, fwd_send.at[o]).wait_recv()
-
-    def turn_refs(gp, carry):
-        for u in range(units):
-            for e in range(unit_devs):
-                y = refs[u * unit_devs + e, gp].astype(jnp.float32)
+    lanes = pp * S1
+
+    def score_copy(u, src, slot, target, o):
+        return pltpu.make_async_remote_copy(
+            src_ref=scores.at[u, src], dst_ref=got.at[u, slot], send_sem=score_send.at[u, o],
+            recv_sem=score_recv.at[u, slot], device_id={"blk": target}, device_id_type=MESH,
+        )
+
+    fwd, score_copies = [], []
+    for i in range(chips):
+        u = lax.rem(chip + chips - i, chips)
+        if i == 0:
+            ref_copy(sibling, sibling, ref_send.at[chips - 1]).wait_recv()
+        else:
+            slot = u * 2 + core
+            ref_copy(slot, slot, ref_send.at[i - 1]).wait_recv()
+            copy = ref_copy(slot, sibling, fwd_send.at[i - 1])
+            copy.start()
+            fwd.append(copy)
+            ref_copy(u * 2 + 1 - core, sibling, fwd_send.at[i - 1]).wait_recv()
+        norm[...] = jnp.zeros_like(norm)
+        scores[u] = jnp.zeros(scores.shape[1:], jnp.float32)
+
+        def body(gp, carry, u=u):
+            for e in range(2):
+                y = refs[u * 2 + e, gp].astype(jnp.float32)
                 for h in range(2):
-                    flat[u, h, e * own : (e + 1) * own, :] = y[h * own : (h + 1) * own, :]
+                    flat[h, e * own : (e + 1) * own, :] = y[h * own : (h + 1) * own, :]
             for h in range(2):
-                y = flat[u, h]
+                y = flat[h]
                 half = 0.5 * jnp.sum(y * y, axis=1, keepdims=True)
-                norm[u] += jnp.broadcast_to(half, (UNIT, norm.shape[2]))
+                norm[...] += jnp.broadcast_to(half, norm.shape)
                 for s2 in range(S2):
-                    at = u * S2 * UNIT + s2 * UNIT
-                    turned[gp * 2 + h, at : at + UNIT, :] = roll_cycles(
+                    turned[h, s2 * unit : (s2 + 1) * unit, :] = roll_cycles(
                         y, -step * S1 * s2, angles
                     ).astype(jnp.bfloat16)
-        return carry
-
-    lax.fori_loop(0, groups // 2, turn_refs, 0)
-
-    lanes = pp * S1
-
-    def score_pair(which):
-        first = which * 2
-        for i in range(2):
-            for u in range(units):
-                for s2 in range(S2):
-                    at = u * S2 * UNIT + s2 * UNIT
-                    scores[first + i, at : at + UNIT, :] = -norm[u]
-
-        def body(g, carry):
-            cols = rolled[g, pl.ds(pl.multiple_of(which * 2 * lanes, 2 * lanes), 2 * lanes), :]
-            prod = lax.dot_general(turned[g], cols, NT, preferred_element_type=jnp.float32)
-            for i in range(2):
-                scores[first + i] += prod[:, i * lanes : (i + 1) * lanes]
+            for h in range(2):
+                prod = lax.dot_general(
+                    turned[h], rolled[gp * 2 + h], NT, preferred_element_type=jnp.float32
+                )
+                for j in range(n_blk):
+                    scores[u, j] += prod[:, j * lanes : (j + 1) * lanes]
             return carry
 
-        lax.fori_loop(0, groups, body, 0)
-
-    def score_copy(src, slot, target, o):
-        return pltpu.make_async_remote_copy(
-            src_ref=scores.at[src], dst_ref=got.at[slot], send_sem=score_send.at[o],
-            recv_sem=score_recv.at[slot], device_id={"blk": target}, device_id_type=MESH,
-        )
-
-    score_copies = [score_copy(b, blk, b, o) for o, b in enumerate(blk_peers)]
-    score_pair(1 - pair)
-    score_copies[1].start()
-    score_copies[0].start()
-    score_pair(pair)
-    score_copies[2].start()
-    for o in (2, 0, 1):
-        b = blk_peers[o]
-        score_copy(b, b, b, o).wait_recv()
-    total = scores[blk]
-    for b in blk_peers:
-        total = total + got[b]
+        lax.fori_loop(0, groups // 2, body, 0)
+        for j in range(n_blk):
+            for s2 in range(S2):
+                scores[u, j, s2 * unit : (s2 + 1) * unit, :] -= norm[...]
+        copies = [score_copy(u, b, blk, b, o) for o, b in enumerate(blk_peers)]
+        for o in (1, 0, 2):
+            copies[o].start()
+        score_copies += copies
+
+    for u in range(chips):
+        for o, b in enumerate(blk_peers):
+            score_copy(u, b, b, b, o).wait_recv()
+    total = jnp.concatenate(
+        [
+            functools.reduce(jnp.add, [got[u, b] for b in blk_peers], scores[u, blk])
+            for u in range(chips)
+        ],
+        axis=0,
+    )
     logits = total * prec_ref[blk][0:1, :]
     top = jnp.broadcast_to(jnp.max(logits, axis=0, keepdims=True), (8, lanes))
     top = spread_lanes(jnp.maximum, top, pp)[0:1, :]
@@ -222,16 +240,16 @@
                 spread = jnp.dot(
                     w, rolled[q * per_piece + gi], preferred_element_type=jnp.float32
                 )
-                for u in range(units):
-                    base = u * S2 * UNIT
-                    running = spread[base + (S2 - 1) * UNIT : base + S2 * UNIT, :]
+                for u in range(chips):
+                    base = u * span
+                    running = spread[base + (S2 - 1) * unit : base + span, :]
                     for s2 in reversed(range(S2 - 1)):
                         running = (
                             roll_cycles(running, step * S1, angles)
-                            + spread[base + s2 * UNIT : base + (s2 + 1) * UNIT, :]
+                            + spread[base + s2 * unit : base + (s2 + 1) * unit, :]
                         )
-                    for k in range(unit_devs):
-                        d = u * unit_devs + k
+                    for k in range(2):
+                        d = u * 2 + k
                         parts[d % 2, q, d // 2, gi] = running[k * own : (k + 1) * own, :]
                 return carry
 
@@ -278,15 +296,14 @@
     groups = cycles // G
     wide = G * angles
     chips = n_dom // 2
-    units = classes // UNIT
+    unit = 2 * own
     pp = particles // n_blk
     lhs = S2 * classes
     rhs = S1 * particles
     per_piece = groups // PIECES
 
-    grouped = images.reshape(particles, groups, wide).transpose(1, 0, 2)
-    store = ref_store[0].reshape(blocks, per_block, groups, wide).transpose(0, 2, 1, 3)
-    store = store.reshape(blocks, groups * per_block, wide)
+    flat_images = images.reshape(particles * cycles, angles)
+    store = ref_store.reshape(blocks, per_block * cycles, angles)
     prec = jnp.tile(precision.reshape(n_blk, 1, pp), (1, 8, S1))
 
     vmem = pl.BlockSpec(memory_space=pltpu.VMEM)
@@ -299,21 +316,23 @@
         out_specs=vmem,
         out_shape=jax.ShapeDtypeStruct((own, cycles, angles), f32),
         scratch_shapes=[
+            pltpu.VMEM((angles // LANES, particles * cycles, LANES), f32),
+            pltpu.VMEM((angles // LANES, own * cycles, LANES), f32),
             pltpu.VMEM((groups // 2, 2 * own, wide), f32),
             pltpu.VMEM((n_dom, groups // 2, 2 * own, wide), bf16),
             pltpu.VMEM((groups, rhs, wide), bf16),
-            pltpu.VMEM((groups, lhs, wide), bf16),
-            pltpu.VMEM((units, 2, UNIT, wide), f32),
-            pltpu.VMEM((units, UNIT, pp * S1), f32),
-            pltpu.VMEM((n_blk, lhs, pp * S1), f32),
-            pltpu.VMEM((n_blk, lhs, pp * S1), f32),
+            pltpu.VMEM((2, S2 * unit, wide), bf16),
+            pltpu.VMEM((2, unit, wide), f32),
+            pltpu.VMEM((unit, pp * S1), f32),
+            pltpu.VMEM((chips, n_blk, S2 * unit, pp * S1), f32),
+            pltpu.VMEM((chips, n_blk, S2 * unit, pp * S1), f32),
             pltpu.VMEM((n_blk, lhs, pp * S1), bf16),
             pltpu.VMEM((2, PIECES, chips, per_piece, own, wide), f32),
             pltpu.VMEM((PIECES, chips, per_piece, own, wide), f32),
             pltpu.VMEM((PIECES, chips, per_piece * own, wide), bf16),
             pltpu.VMEM((PIECES, chips, per_piece * own, wide), bf16),
             dma((chips,)), dma((n_dom,)), dma((chips,)),
-            dma((n_blk,)), dma((n_blk,)), dma((n_blk,)), dma((n_blk,)),
+            dma((chips, n_blk)), dma((chips, n_blk)), dma((n_blk,)), dma((n_blk,)),
             dma((PIECES,)), dma((PIECES,)), dma((PIECES, chips)), dma((PIECES, chips)),
         ],
         compiler_params=pltpu.CompilerParams(
@@ -323,7 +342,7 @@
             flops=4 * lhs * rhs * groups * wide, bytes_accessed=4 * 1024 * 1024, transcendentals=0
         ),
         name="fused",
-    )(block_owner, class_gain, prec, grouped, store)
+    )(block_owner, class_gain, prec, flat_images, store)
     return out.reshape(1, owned, per_block, cycles, angles)
 
 

time: 73.1 us -> 63.5 us (0.87)
  Pallas kernels: 65.2 us -> 59.9 us
  local copies, waits for them, and re-layouts: 7.6 us -> 3.42 us
    pallas_call x1, Pallas kernels: 65.2 us -> 59.9 us  [shards(): pl.pallas_call(functools.partial(kernel, n_dom, n_blk, angles, per_block,...]
    another operation x2 -> x0, local copies, waits for them, and re-layouts: 2.59 us -> none  [shards(): ref_store[0].reshape(blocks, per_block, groups, wide).transpose(0, 2, 1, 3)]
    reshape x3 -> x0, local copies, waits for them, and re-layouts: 2.34 us -> none  [the longest x2 1.23 us: shards(): grouped = images.reshape(particles, groups, wide).transpose(1, 0, 2)]
    unnamed x9, local copies, waits for them, and re-layouts: 2.5 us -> 3.24 us
where the time goes in v3:
time: 63.5 us; the launch traced here: 63.3 us
  Pallas kernels  59.9 us (94%)
  local copies, waits for them, and re-layouts  3.42 us (5%)
    pallas_call x1, Pallas kernels, shards(): pl.pallas_call(functools.partial(kernel, n_dom, n_blk, angles, per_block,...  59.9 us
    unnamed x9, local copies, waits for them, and re-layouts  3.24 us

profile of v3, /device:TPU:0, one launch (start us, length us, event | category | flops | bytes accessed | tf_op | source)
XLA Modules:
  0.0 63.3 jit_solution(633080234400970581)
XLA Ops:
  0.0 0.0 copy-start.3
  0.0 0.7 %copy-done.3 = f32[64]{0:T(128)S(1)} copy-done((f32[64]{0:T(128)S(1)}, f32[64]{0:T(128)}, u32[]{:S(2)}) %copy-start.3) | copy-done | bytes 280
  0.7 0.1 tile.12
  0.7 0.1 tile.14
  0.8 0.0 copy-start.1
  0.8 0.0 copy-start.2
  0.8 0.6 %copy-done.1 = s32[16]{0:T(128)S(1)} copy-done((s32[16]{0:T(128)S(1)}, s32[16]{0:T(128)}, u32[]{:S(2)}) %copy-start.1) | copy-done | bytes 88
  1.5 0.0 copy-done.2
  1.5 0.0 copy-start
  1.5 1.2 %copy-done = bf16[64,32,256]{2,1,0:T(8,128)(2,1)S(1)} copy-done((bf16[64,32,256]{2,1,0:T(8,128)(2,1)S(1)}, bf16[64,32,256]{2,1,0:T(8,128)(2,1)}, u32[]{:S(2)}) %copy-start) | copy-done | bytes 1048600
  2.7 59.9 %fused.1 = f32[8,32,256]{2,1,0:T(8,128)S(1)} custom-call(s32[16]{0:T(128)S(1)} %copy-done.1, f32[64]{0:T(128)S(1)} %copy-done.2, f32[4,8,128]{2,1,0:T(8,128)S(1)} %tile.15.prec_ref, bf16[2048,256]{1,0:T(8,128)(2,1)S(1)} %bitcast.4, bf16[16,128,256]{2,1,0:T(8,128)(2,1)} %bitcast.5), custom_call_target="tpu_custom_call" | custom-call | flops 8589934592 | bytes 4194304 | tf_op jit(solution)/shard_map/fused/pallas_call | solution.py:313
  62.6 0.7 %copy.7 = f32[1,2,4,32,256]{4,3,2,1,0:T(8,128)} copy(f32[1,2,4,32,256]{4,3,2,1,0:T(8,128)S(1)} %bitcast.3) | data formatting | bytes 524288
  (2 shorter events, 0.0 us)
Async XLA Ops:
  0.0 0.7 %copy-start.3 = (f32[64]{0:T(128)S(1)}, f32[64]{0:T(128)}, u32[]{:S(2)}) copy-start(f32[64]{0:T(128)} %param.9) | copy-start | bytes 772
  0.8 0.7 %copy-start.1 = (s32[16]{0:T(128)S(1)}, s32[16]{0:T(128)}, u32[]{:S(2)}) copy-start(s32[16]{0:T(128)} %owner_ref.1) | copy-start | bytes 196
  0.8 0.7 %copy-start.2 = (f32[64]{0:T(128)S(1)}, f32[64]{0:T(128)}, u32[]{:S(2)}) copy-start(f32[64]{0:T(128)} %gain_ref.1) | copy-start | bytes 772
  1.5 1.2 %copy-start = (bf16[64,32,256]{2,1,0:T(8,128)(2,1)S(1)}, bf16[64,32,256]{2,1,0:T(8,128)(2,1)}, u32[]{:S(2)}) copy-start(bf16[64,32,256]{2,1,0:T(8,128)(2,1)} %param.5) | copy-start | bytes 3145732

commit v4 on v3

--- a/solution.py
+++ b/solution.py
@@ -27,6 +27,15 @@
     return jnp.concatenate(parts, axis=1)
 
 
+def swap_halves(x, angles):
+    half = angles // 2
+    parts = []
+    for c in range(x.shape[1] // angles):
+        parts.append(x[:, c * angles + half : (c + 1) * angles])
+        parts.append(x[:, c * angles : c * angles + half])
+    return jnp.concatenate(parts, axis=1)
+
+
 def every(ref, start, count, stride):
     return jnp.concatenate(
         [ref[h, pl.ds(start, count, stride=stride), :] for h in range(ref.shape[0])], axis=1
@@ -43,10 +52,10 @@
 
 def kernel(
     n_dom, n_blk, angles, per_block, owned,
-    owner_ref, gain_ref, prec_ref, img_ref, store_ref, out_ref,
-    imgf, blockf, minef, refs, rolled, turned, flat, norm, scores, got, weights, parts, sib, zout, zin,
+    owner_ref, gain_ref, prec_ref, img_hbm, store_hbm, out_ref,
+    img_ref, store_ref, imgf, blockf, minef, refs, rolled, turned, flat, norm, scores, got, weights, whole, parts, sib, zout, zin,
     ref_send, ref_recv, fwd_send, score_send, score_recv, w_send, w_recv,
-    sib_send, sib_recv, z_send, z_recv,
+    sib_send, sib_recv, z_send, z_recv, local,
 ):
     step = angles // S
     own = owned * per_block
@@ -69,6 +78,10 @@
     pair = blk // 2
     blk_peers = [(1 - pair) * 2, (1 - pair) * 2 + 1, pair * 2 + 1 - blk % 2]
 
+    store_in = pltpu.make_async_copy(store_hbm, store_ref, local.at[0])
+    img_in = pltpu.make_async_copy(img_hbm, img_ref, local.at[1])
+    store_in.start()
+    img_in.start()
     barrier = pltpu.get_barrier_semaphore()
     for c in far:
         pl.semaphore_signal(barrier, inc=1, device_id={"dom": c * 2 + core}, device_id_type=MESH)
@@ -84,6 +97,7 @@
             take = jnp.logical_and(hit == 1, seen == j)
             picks[j] = jnp.where(take, jnp.int32(b), picks[j])
         seen = seen + hit
+    store_in.wait()
     for j in range(owned):
         block = store_ref[picks[j]].astype(jnp.float32)
         for i in range(per_block):
@@ -113,6 +127,8 @@
     for copy in out_copies:
         copy.start()
 
+    img_in.wait()
+
     def widen(i, carry):
         at = pl.ds(pl.multiple_of(i * 256, 256), 256)
         for h in range(halves):
@@ -123,9 +139,9 @@
 
     def roll_images(g, carry):
         for rr in range(G):
-            x = every(imgf, g * G + rr, particles, cycles)
+            x = every(imgf, g * G + rr, particles, cycles).astype(jnp.bfloat16)
             for s1 in range(S1):
-                r = roll_cycles(x, step * s1, angles).astype(jnp.bfloat16)
+                r = roll_cycles(x, step * s1, angles)
                 for j in range(n_blk):
                     at = j * pp * S1 + s1 * pp
                     rolled[g, at : at + pp, rr * angles : (rr + 1) * angles] = r[
@@ -166,10 +182,12 @@
                 y = flat[h]
                 half = 0.5 * jnp.sum(y * y, axis=1, keepdims=True)
                 norm[...] += jnp.broadcast_to(half, norm.shape)
-                for s2 in range(S2):
-                    turned[h, s2 * unit : (s2 + 1) * unit, :] = roll_cycles(
-                        y, -step * S1 * s2, angles
-                    ).astype(jnp.bfloat16)
+                y16 = y.astype(jnp.bfloat16)
+                for s2 in range(S2 // 2):
+                    t = roll_cycles(y16, -step * S1 * s2, angles)
+                    turned[h, s2 * unit : (s2 + 1) * unit, :] = t
+                    at = (s2 + S2 // 2) * unit
+                    turned[h, at : at + unit, :] = swap_halves(t, angles)
             for h in range(2):
                 prod = lax.dot_general(
                     turned[h], rolled[gp * 2 + h], NT, preferred_element_type=jnp.float32
@@ -197,7 +215,11 @@
         ],
         axis=0,
     )
-    logits = total * prec_ref[blk][0:1, :]
+    lane = lax.broadcasted_iota(jnp.int32, (8, lanes), 1) & (pp - 1)
+    prec = jnp.zeros((8, lanes), jnp.float32)
+    for i in range(pp):
+        prec = jnp.where(lane == i, prec_ref[blk * pp + i], prec)
+    logits = total * prec[0:1, :]
     top = jnp.broadcast_to(jnp.max(logits, axis=0, keepdims=True), (8, lanes))
     top = spread_lanes(jnp.maximum, top, pp)[0:1, :]
     e = jnp.exp(logits - top)
@@ -217,6 +239,8 @@
     for o, b in enumerate(blk_peers):
         w_copy(b, b, o).wait_recv()
 
+    for j in range(n_blk):
+        whole[:, j * lanes : (j + 1) * lanes] = weights[j]
     per_piece = groups // PIECES
 
     def sib_copy(q, which):
@@ -236,18 +260,21 @@
         if q < PIECES:
 
             def body(gi, carry, q=q):
-                w = jnp.concatenate([weights[j] for j in range(n_blk)], axis=1)
                 spread = jnp.dot(
-                    w, rolled[q * per_piece + gi], preferred_element_type=jnp.float32
+                    whole[...], rolled[q * per_piece + gi], preferred_element_type=jnp.float32
                 )
                 for u in range(chips):
                     base = u * span
-                    running = spread[base + (S2 - 1) * unit : base + span, :]
-                    for s2 in reversed(range(S2 - 1)):
-                        running = (
-                            roll_cycles(running, step * S1, angles)
-                            + spread[base + s2 * unit : base + (s2 + 1) * unit, :]
+                    fold = [
+                        spread[base + s2 * unit : base + (s2 + 1) * unit, :]
+                        + swap_halves(
+                            spread[base + span // 2 + s2 * unit :][:unit, :], angles
                         )
+                        for s2 in range(S2 // 2)
+                    ]
+                    running = fold[-1]
+                    for s2 in reversed(range(S2 // 2 - 1)):
+                        running = roll_cycles(running, step * S1, angles) + fold[s2]
                     for k in range(2):
                         d = u * 2 + k
                         parts[d % 2, q, d // 2, gi] = running[k * own : (k + 1) * own, :]
@@ -304,18 +331,20 @@
 
     flat_images = images.reshape(particles * cycles, angles)
     store = ref_store.reshape(blocks, per_block * cycles, angles)
-    prec = jnp.tile(precision.reshape(n_blk, 1, pp), (1, 8, S1))
 
     vmem = pl.BlockSpec(memory_space=pltpu.VMEM)
     smem = pl.BlockSpec(memory_space=pltpu.SMEM)
+    hbm = pl.BlockSpec(memory_space=pl.ANY)
     bf16, f32 = jnp.bfloat16, jnp.float32
     dma = pltpu.SemaphoreType.DMA
     out = pl.pallas_call(
         functools.partial(kernel, n_dom, n_blk, angles, per_block, owned),
-        in_specs=[smem, smem, vmem, vmem, vmem],
+        in_specs=[smem, smem, smem, hbm, hbm],
         out_specs=vmem,
         out_shape=jax.ShapeDtypeStruct((own, cycles, angles), f32),
         scratch_shapes=[
+            pltpu.VMEM((particles * cycles, angles), bf16),
+            pltpu.VMEM((blocks, per_block * cycles, angles), bf16),
             pltpu.VMEM((angles // LANES, particles * cycles, LANES), f32),
             pltpu.VMEM((angles // LANES, own * cycles, LANES), f32),
             pltpu.VMEM((groups // 2, 2 * own, wide), f32),
@@ -327,13 +356,14 @@
             pltpu.VMEM((chips, n_blk, S2 * unit, pp * S1), f32),
             pltpu.VMEM((chips, n_blk, S2 * unit, pp * S1), f32),
             pltpu.VMEM((n_blk, lhs, pp * S1), bf16),
+            pltpu.VMEM((lhs, rhs), bf16),
             pltpu.VMEM((2, PIECES, chips, per_piece, own, wide), f32),
             pltpu.VMEM((PIECES, chips, per_piece, own, wide), f32),
             pltpu.VMEM((PIECES, chips, per_piece * own, wide), bf16),
             pltpu.VMEM((PIECES, chips, per_piece * own, wide), bf16),
             dma((chips,)), dma((n_dom,)), dma((chips,)),
             dma((chips, n_blk)), dma((chips, n_blk)), dma((n_blk,)), dma((n_blk,)),
-            dma((PIECES,)), dma((PIECES,)), dma((PIECES, chips)), dma((PIECES, chips)),
+            dma((PIECES,)), dma((PIECES,)), dma((PIECES, chips)), dma((PIECES, chips)), dma((2,)),
         ],
         compiler_params=pltpu.CompilerParams(
             collective_id=0, has_side_effects=True, vmem_limit_bytes=52 * 1024 * 1024
@@ -342,7 +372,7 @@
             flops=4 * lhs * rhs * groups * wide, bytes_accessed=4 * 1024 * 1024, transcendentals=0
         ),
         name="fused",
-    )(block_owner, class_gain, prec, flat_images, store)
+    )(block_owner, class_gain, precision, flat_images, store)
     return out.reshape(1, owned, per_block, cycles, angles)
 
 

time: 63.5 us -> 60.9 us (0.959)
  Pallas kernels: 59.9 us -> 58 us
  local copies, waits for them, and re-layouts: 3.42 us -> 2.61 us
    pallas_call x1, Pallas kernels: 59.9 us -> 58 us  [shards(): pl.pallas_call(functools.partial(kernel, n_dom, n_blk, angles, per_block,...]
where the time goes in v4:
time: 60.9 us; the launch traced here: 60.7 us
  Pallas kernels  58 us (95%)
  local copies, waits for them, and re-layouts  2.61 us (4%)
    pallas_call x1, Pallas kernels, shards(): pl.pallas_call(functools.partial(kernel, n_dom, n_blk, angles, per_block,...  58 us
    unnamed x9, local copies, waits for them, and re-layouts  2.61 us

profile of v4, /device:TPU:0, one launch (start us, length us, event | category | flops | bytes accessed | tf_op | source)
XLA Modules:
  0.0 60.7 jit_solution(9254197760989411440)
XLA Ops:
  0.0 0.0 copy-start.1
  0.0 0.0 copy-start.2
  0.0 0.0 copy-start.3
  0.0 0.6 %copy-done.1 = s32[16]{0:T(128)S(1)} copy-done((s32[16]{0:T(128)S(1)}, s32[16]{0:T(128)}, u32[]{:S(2)}) %copy-start.1) | copy-done | bytes 88
  0.7 0.0 copy-done.2
  0.7 0.0 copy-done.3
  0.7 0.0 copy-start
  0.7 1.2 %copy-done = bf16[64,32,256]{2,1,0:T(8,128)(2,1)S(1)} copy-done((bf16[64,32,256]{2,1,0:T(8,128)(2,1)S(1)}, bf16[64,32,256]{2,1,0:T(8,128)(2,1)}, u32[]{:S(2)}) %copy-start) | copy-done | bytes 1048600
  1.9 58.0 %fused.1 = f32[8,32,256]{2,1,0:T(8,128)S(1)} custom-call(s32[16]{0:T(128)S(1)} %copy-done.1, f32[64]{0:T(128)S(1)} %copy-done.2, f32[64]{0:T(128)S(1)} %copy-done.3, bf16[2048,256]{1,0:T(8,128)(2,1)S(1)} %bitcast.4, bf16[16,128,256]{2,1,0:T(8,128)(2,1)} %bitcast.5), custom_call_target="tpu_custom_call" | custom-call | flops 8589934592 | bytes 4194304 | tf_op jit(solution)/shard_map/fused/pallas_call | solution.py:340
  60.0 0.7 %copy.7 = f32[1,2,4,32,256]{4,3,2,1,0:T(8,128)} copy(f32[1,2,4,32,256]{4,3,2,1,0:T(8,128)S(1)} %bitcast.3) | data formatting | bytes 524288
Async XLA Ops:
  0.0 0.7 %copy-start.1 = (s32[16]{0:T(128)S(1)}, s32[16]{0:T(128)}, u32[]{:S(2)}) copy-start(s32[16]{0:T(128)} %owner_ref.1) | copy-start | bytes 196
  0.0 0.7 %copy-start.2 = (f32[64]{0:T(128)S(1)}, f32[64]{0:T(128)}, u32[]{:S(2)}) copy-start(f32[64]{0:T(128)} %gain_ref.1) | copy-start | bytes 772
  0.0 0.7 %copy-start.3 = (f32[64]{0:T(128)S(1)}, f32[64]{0:T(128)}, u32[]{:S(2)}) copy-start(f32[64]{0:T(128)} %prec_ref.1) | copy-start | bytes 772
  0.7 1.2 %copy-start = (bf16[64,32,256]{2,1,0:T(8,128)(2,1)S(1)}, bf16[64,32,256]{2,1,0:T(8,128)(2,1)}, u32[]{:S(2)}) copy-start(bf16[64,32,256]{2,1,0:T(8,128)(2,1)} %param.5) | copy-start | bytes 3145732

commit v5 on v4

--- a/solution.py
+++ b/solution.py
@@ -52,8 +52,8 @@
 
 def kernel(
     n_dom, n_blk, angles, per_block, owned,
-    owner_ref, gain_ref, prec_ref, img_hbm, store_hbm, out_ref,
-    img_ref, store_ref, imgf, blockf, minef, refs, rolled, turned, flat, norm, scores, got, weights, whole, parts, sib, zout, zin,
+    owner_hbm, gain_hbm, prec_hbm, img_hbm, store_hbm, out_ref,
+    owner_ref, gain_ref, prec_ref, img_ref, store_ref, imgf, blockf, minef, refs, rolled, turned, flat, norm, scores, got, weights, whole, parts, sib, zout, zin,
     ref_send, ref_recv, fwd_send, score_send, score_recv, w_send, w_recv,
     sib_send, sib_recv, z_send, z_recv, local,
 ):
@@ -80,6 +80,13 @@
 
     store_in = pltpu.make_async_copy(store_hbm, store_ref, local.at[0])
     img_in = pltpu.make_async_copy(img_hbm, img_ref, local.at[1])
+    small_in = [
+        pltpu.make_async_copy(owner_hbm, owner_ref, local.at[2]),
+        pltpu.make_async_copy(gain_hbm, gain_ref, local.at[3]),
+        pltpu.make_async_copy(prec_hbm, prec_ref, local.at[4]),
+    ]
+    for copy in small_in:
+        copy.start()
     store_in.start()
     img_in.start()
     barrier = pltpu.get_barrier_semaphore()
@@ -89,6 +96,8 @@
     for b in blk_peers:
         pl.semaphore_signal(barrier, inc=1, device_id={"blk": b}, device_id_type=MESH)
 
+    for copy in small_in:
+        copy.wait()
     picks = [jnp.int32(0)] * owned
     seen = jnp.int32(0)
     for b in range(blocks):
@@ -225,46 +234,70 @@
     e = jnp.exp(logits - top)
     mass = jnp.broadcast_to(jnp.sum(e, axis=0, keepdims=True), (8, lanes))
     mass = spread_lanes(jnp.add, mass, pp)[0:1, :]
-    weights[blk] = (e * (1.0 / mass)).astype(jnp.bfloat16)
-
-    def w_copy(slot, target, o):
+    w = (e * (1.0 / mass)).astype(jnp.bfloat16)
+    for u in range(chips):
+        weights[u, blk] = w[u * span : (u + 1) * span, :]
+
+    def w_copy(u, slot, target, o):
         return pltpu.make_async_remote_copy(
-            src_ref=weights.at[slot], dst_ref=weights.at[slot], send_sem=w_send.at[o],
-            recv_sem=w_recv.at[slot], device_id={"blk": target}, device_id_type=MESH,
-        )
-
-    w_copies = [w_copy(blk, b, o) for o, b in enumerate(blk_peers)]
-    for o in (1, 0, 2):
-        w_copies[o].start()
-    for o, b in enumerate(blk_peers):
-        w_copy(b, b, o).wait_recv()
-
-    for j in range(n_blk):
-        whole[:, j * lanes : (j + 1) * lanes] = weights[j]
+            src_ref=weights.at[u, slot], dst_ref=weights.at[u, slot], send_sem=w_send.at[u, o],
+            recv_sem=w_recv.at[u, slot], device_id={"blk": target}, device_id_type=MESH,
+        )
+
+    order = far + [chip]
+    w_copies = []
+    for u in order:
+        copies = [w_copy(u, blk, b, o) for o, b in enumerate(blk_peers)]
+        for o in (1, 0, 2):
+            copies[o].start()
+        w_copies += copies
+
     per_piece = groups // PIECES
-
-    def sib_copy(q, which):
+    part = chips // 2
+
+    def sib_copy(h, q, which):
         return pltpu.make_async_remote_copy(
-            src_ref=parts.at[which, q], dst_ref=sib.at[q], send_sem=sib_send.at[q],
-            recv_sem=sib_recv.at[q], device_id={"dom": sibling}, device_id_type=MESH,
-        )
-
-    def z_copy(q, src, slot, target, o):
+            src_ref=parts.at[which, h, q], dst_ref=sib.at[h, q], send_sem=sib_send.at[h, q],
+            recv_sem=sib_recv.at[h, q], device_id={"dom": sibling}, device_id_type=MESH,
+        )
+
+    def z_copy(q, src, slot, target):
         return pltpu.make_async_remote_copy(
-            src_ref=zout.at[q, src], dst_ref=zin.at[q, slot], send_sem=z_send.at[q, o],
+            src_ref=zout.at[q, src], dst_ref=zin.at[q, slot], send_sem=z_send.at[q, src],
             recv_sem=z_recv.at[q, slot], device_id={"dom": target * 2 + core}, device_id_type=MESH,
         )
 
     sib_copies, z_copies = [], []
-    for q in range(PIECES + 1):
-        if q < PIECES:
-
-            def body(gi, carry, q=q):
+
+    def finish(h, q):
+        sib_copy(h, q, 1 - core).wait_recv()
+        for i in range(part):
+            at = h * part + i
+            both = parts[core, h, q, i] + sib[h, q, i]
+            if at == chips - 1:
+                parts[core, h, q, i] = both
+                continue
+            zout[q, at] = both.reshape(per_piece * own, wide).astype(jnp.bfloat16)
+            copy = z_copy(q, at, chip, order[at])
+            copy.start()
+            z_copies.append(copy)
+
+    last = None
+    for h in range(2):
+        for i in range(part):
+            u = order[h * part + i]
+            for o, b in enumerate(blk_peers):
+                w_copy(u, b, b, o).wait_recv()
+            for j in range(n_blk):
+                whole[i * span : (i + 1) * span, j * lanes : (j + 1) * lanes] = weights[u, j]
+        for q in range(PIECES):
+
+            def body(gi, carry, h=h, q=q):
                 spread = jnp.dot(
                     whole[...], rolled[q * per_piece + gi], preferred_element_type=jnp.float32
                 )
-                for u in range(chips):
-                    base = u * span
+                for i in range(part):
+                    base = i * span
                     fold = [
                         spread[base + s2 * unit : base + (s2 + 1) * unit, :]
                         + swap_halves(
@@ -276,30 +309,22 @@
                     for s2 in reversed(range(S2 // 2 - 1)):
                         running = roll_cycles(running, step * S1, angles) + fold[s2]
                     for k in range(2):
-                        d = u * 2 + k
-                        parts[d % 2, q, d // 2, gi] = running[k * own : (k + 1) * own, :]
+                        parts[k, h, q, i, gi] = running[k * own : (k + 1) * own, :]
                 return carry
 
             lax.fori_loop(0, per_piece, body, 0)
-            copy = sib_copy(q, 1 - core)
+            copy = sib_copy(h, q, 1 - core)
             copy.start()
             sib_copies.append(copy)
-        if q >= 1:
-            p = q - 1
-            sib_copy(p, 1 - core).wait_recv()
-            for c in range(chips):
-                both = parts[core, p, c] + sib[p, c]
-                parts[core, p, c] = both
-                zout[p, c] = both.reshape(per_piece * own, wide).astype(jnp.bfloat16)
-            for o, c in enumerate(far):
-                copy = z_copy(p, c, chip, c, o)
-                copy.start()
-                z_copies.append(copy)
+            if last is not None:
+                finish(*last)
+            last = (h, q)
+    finish(*last)
 
     for q in range(PIECES):
-        total = parts[core, q, chip].reshape(per_piece * own, wide)
-        for o, c in enumerate(far):
-            z_copy(q, c, c, c, o).wait_recv()
+        total = parts[core, 1, q, part - 1].reshape(per_piece * own, wide)
+        for c in far:
+            z_copy(q, 0, c, c).wait_recv()
             total = total + zin[q, c].astype(jnp.float32)
         for gi in range(per_piece):
             for rr in range(G):
@@ -333,16 +358,18 @@
     store = ref_store.reshape(blocks, per_block * cycles, angles)
 
     vmem = pl.BlockSpec(memory_space=pltpu.VMEM)
-    smem = pl.BlockSpec(memory_space=pltpu.SMEM)
     hbm = pl.BlockSpec(memory_space=pl.ANY)
     bf16, f32 = jnp.bfloat16, jnp.float32
     dma = pltpu.SemaphoreType.DMA
     out = pl.pallas_call(
         functools.partial(kernel, n_dom, n_blk, angles, per_block, owned),
-        in_specs=[smem, smem, smem, hbm, hbm],
+        in_specs=[hbm] * 5,
         out_specs=vmem,
         out_shape=jax.ShapeDtypeStruct((own, cycles, angles), f32),
         scratch_shapes=[
+            pltpu.SMEM((blocks,), jnp.int32),
+            pltpu.SMEM((classes,), f32),
+            pltpu.SMEM((particles,), f32),
             pltpu.VMEM((particles * cycles, angles), bf16),
             pltpu.VMEM((blocks, per_block * cycles, angles), bf16),
             pltpu.VMEM((angles // LANES, particles * cycles, LANES), f32),
@@ -355,18 +382,18 @@
             pltpu.VMEM((unit, pp * S1), f32),
             pltpu.VMEM((chips, n_blk, S2 * unit, pp * S1), f32),
             pltpu.VMEM((chips, n_blk, S2 * unit, pp * S1), f32),
-            pltpu.VMEM((n_blk, lhs, pp * S1), bf16),
-            pltpu.VMEM((lhs, rhs), bf16),
-            pltpu.VMEM((2, PIECES, chips, per_piece, own, wide), f32),
-            pltpu.VMEM((PIECES, chips, per_piece, own, wide), f32),
+            pltpu.VMEM((chips, n_blk, S2 * unit, pp * S1), bf16),
+            pltpu.VMEM((lhs // 2, rhs), bf16),
+            pltpu.VMEM((2, 2, PIECES, chips // 2, per_piece, own, wide), f32),
+            pltpu.VMEM((2, PIECES, chips // 2, per_piece, own, wide), f32),
             pltpu.VMEM((PIECES, chips, per_piece * own, wide), bf16),
             pltpu.VMEM((PIECES, chips, per_piece * own, wide), bf16),
             dma((chips,)), dma((n_dom,)), dma((chips,)),
-            dma((chips, n_blk)), dma((chips, n_blk)), dma((n_blk,)), dma((n_blk,)),
-            dma((PIECES,)), dma((PIECES,)), dma((PIECES, chips)), dma((PIECES, chips)), dma((2,)),
+            dma((chips, n_blk)), dma((chips, n_blk)), dma((chips, n_blk)), dma((chips, n_blk)),
+            dma((2, PIECES)), dma((2, PIECES)), dma((PIECES, chips)), dma((PIECES, chips)), dma((5,)),
         ],
         compiler_params=pltpu.CompilerParams(
-            collective_id=0, has_side_effects=True, vmem_limit_bytes=52 * 1024 * 1024
+            collective_id=0, has_side_effects=True, vmem_limit_bytes=60 * 1024 * 1024
         ),
         cost_estimate=pl.CostEstimate(
             flops=4 * lhs * rhs * groups * wide, bytes_accessed=4 * 1024 * 1024, transcendentals=0

time: 60.9 us -> 56.5 us (0.928)
  Pallas kernels: 58 us -> 54.4 us
  local copies, waits for them, and re-layouts: 2.61 us -> 1.67 us
    pallas_call x1, Pallas kernels: 58 us -> 54.4 us  [shards(): pl.pallas_call(functools.partial(kernel, n_dom, n_blk, angles, per_block,...]
    unnamed x9 -> x1, local copies, waits for them, and re-layouts: 2.61 us -> 1.67 us
where the time goes in v5:
time: 56.5 us; the launch traced here: 56 us
  Pallas kernels  54.4 us (96%)
  local copies, waits for them, and re-layouts  1.67 us (3%)
    pallas_call x1, Pallas kernels, shards(): pl.pallas_call(functools.partial(kernel, n_dom, n_blk, angles, per_block,...  54.4 us
    unnamed x1, local copies, waits for them, and re-layouts  1.67 us

profile of v5, /device:TPU:0, one launch (start us, length us, event | category | flops | bytes accessed | tf_op | source)
XLA Modules:
  0.0 56.0 jit_solution(8842149120475853117)
XLA Ops:
  0.0 54.4 %fused.1 = f32[8,32,256]{2,1,0:T(8,128)} custom-call(s32[16]{0:T(128)} %owner_hbm.1, f32[64]{0:T(128)} %gain_hbm.1, f32[64]{0:T(128)} %prec_hbm.1, bf16[2048,256]{1,0:T(8,128)(2,1)} %bitcast.4, bf16[16,128,256]{2,1,0:T(8,128)(2,1)} %bitcast.5), custom_call_target="tpu_custom_call" | custom-call | flops 8589934592 | bytes 4194304 | tf_op jit(solution)/shard_map/fused/pallas_call | solution.py:364
  54.4 1.7 %copy.7 = f32[1,2,4,32,256]{4,3,2,1,0:T(8,128)} copy(f32[1,2,4,32,256]{4,3,2,1,0:T(8,128)} %bitcast.3) | data formatting | bytes 524288

commit v6 on v5

--- a/solution.py
+++ b/solution.py
@@ -173,11 +173,6 @@
         if i == 0:
             ref_copy(sibling, sibling, ref_send.at[chips - 1]).wait_recv()
         else:
-            slot = u * 2 + core
-            ref_copy(slot, slot, ref_send.at[i - 1]).wait_recv()
-            copy = ref_copy(slot, sibling, fwd_send.at[i - 1])
-            copy.start()
-            fwd.append(copy)
             ref_copy(u * 2 + 1 - core, sibling, fwd_send.at[i - 1]).wait_recv()
         norm[...] = jnp.zeros_like(norm)
         scores[u] = jnp.zeros(scores.shape[1:], jnp.float32)
@@ -197,15 +192,23 @@
                     turned[h, s2 * unit : (s2 + 1) * unit, :] = t
                     at = (s2 + S2 // 2) * unit
                     turned[h, at : at + unit, :] = swap_halves(t, angles)
-            for h in range(2):
-                prod = lax.dot_general(
-                    turned[h], rolled[gp * 2 + h], NT, preferred_element_type=jnp.float32
-                )
-                for j in range(n_blk):
-                    scores[u, j] += prod[:, j * lanes : (j + 1) * lanes]
+            prod = lax.dot_general(
+                turned[0], rolled[gp * 2], NT, preferred_element_type=jnp.float32
+            ) + lax.dot_general(
+                turned[1], rolled[gp * 2 + 1], NT, preferred_element_type=jnp.float32
+            )
+            for j in range(n_blk):
+                scores[u, j] += prod[:, j * lanes : (j + 1) * lanes]
             return carry
 
-        lax.fori_loop(0, groups // 2, body, 0)
+        lax.fori_loop(0, groups // 4, body, 0)
+        if i < chips - 1:
+            slot = lax.rem(chip + chips - i - 1, chips) * 2 + core
+            ref_copy(slot, slot, ref_send.at[i]).wait_recv()
+            copy = ref_copy(slot, sibling, fwd_send.at[i])
+            copy.start()
+            fwd.append(copy)
+        lax.fori_loop(groups // 4, groups // 2, body, 0)
         for j in range(n_blk):
             for s2 in range(S2):
                 scores[u, j, s2 * unit : (s2 + 1) * unit, :] -= norm[...]

time: 56.5 us -> 55.6 us (0.984)
  Pallas kernels: 54.4 us -> 53.4 us
    pallas_call x1, Pallas kernels: 54.4 us -> 53.4 us  [shards(): pl.pallas_call(functools.partial(kernel, n_dom, n_blk, angles, per_block,...]
where the time goes in v6:
time: 55.6 us; the launch traced here: 55.1 us
  Pallas kernels  53.4 us (96%)
  local copies, waits for them, and re-layouts  1.67 us (3%)
    pallas_call x1, Pallas kernels, shards(): pl.pallas_call(functools.partial(kernel, n_dom, n_blk, angles, per_block,...  53.4 us
    unnamed x1, local copies, waits for them, and re-layouts  1.67 us

profile of v6, /device:TPU:0, one launch (start us, length us, event | category | flops | bytes accessed | tf_op | source)
XLA Modules:
  0.0 55.1 jit_solution(3405390778254516583)
XLA Ops:
  0.0 53.4 %fused.1 = f32[8,32,256]{2,1,0:T(8,128)} custom-call(s32[16]{0:T(128)} %owner_hbm.1, f32[64]{0:T(128)} %gain_hbm.1, f32[64]{0:T(128)} %prec_hbm.1, bf16[2048,256]{1,0:T(8,128)(2,1)} %bitcast.4, bf16[16,128,256]{2,1,0:T(8,128)(2,1)} %bitcast.5), custom_call_target="tpu_custom_call" | custom-call | flops 8589934592 | bytes 4194304 | tf_op jit(solution)/shard_map/fused/pallas_call | solution.py:367
  53.4 1.7 %copy.7 = f32[1,2,4,32,256]{4,3,2,1,0:T(8,128)} copy(f32[1,2,4,32,256]{4,3,2,1,0:T(8,128)} %bitcast.3) | data formatting | bytes 524288

commit v7 on v6

--- a/solution.py
+++ b/solution.py
@@ -315,7 +315,7 @@
                         parts[k, h, q, i, gi] = running[k * own : (k + 1) * own, :]
                 return carry
 
-            lax.fori_loop(0, per_piece, body, 0)
+            lax.fori_loop(0, per_piece, body, 0, unroll=True)
             copy = sib_copy(h, q, 1 - core)
             copy.start()
             sib_copies.append(copy)

time: 55.6 us -> 55.2 us (level)
  Pallas kernels: 53.4 us -> 52.8 us
    pallas_call x1, Pallas kernels: 53.4 us -> 52.8 us  [shards(): pl.pallas_call(functools.partial(kernel, n_dom, n_blk, angles, per_block,...]
where the time goes in v7:
time: 55.2 us; the launch traced here: 54.5 us
  Pallas kernels  52.8 us (96%)
  local copies, waits for them, and re-layouts  1.67 us (3%)
    pallas_call x1, Pallas kernels, shards(): pl.pallas_call(functools.partial(kernel, n_dom, n_blk, angles, per_block,...  52.8 us
    unnamed x1, local copies, waits for them, and re-layouts  1.67 us

profile of v7, /device:TPU:0, one launch (start us, length us, event | category | flops | bytes accessed | tf_op | source)
XLA Modules:
  0.0 54.5 jit_solution(13905487045319464280)
XLA Ops:
  0.0 52.8 %fused.1 = f32[8,32,256]{2,1,0:T(8,128)} custom-call(s32[16]{0:T(128)} %owner_hbm.1, f32[64]{0:T(128)} %gain_hbm.1, f32[64]{0:T(128)} %prec_hbm.1, bf16[2048,256]{1,0:T(8,128)(2,1)} %bitcast.4, bf16[16,128,256]{2,1,0:T(8,128)(2,1)} %bitcast.5), custom_call_target="tpu_custom_call" | custom-call | flops 8589934592 | bytes 4194304 | tf_op jit(solution)/shard_map/fused/pallas_call | solution.py:367
  52.8 1.7 %copy.7 = f32[1,2,4,32,256]{4,3,2,1,0:T(8,128)} copy(f32[1,2,4,32,256]{4,3,2,1,0:T(8,128)} %bitcast.3) | data formatting | bytes 524288
